TPU v7x, 512 devices: a whole 4x4x16 slice. The times are simulated.
512 devices in a mesh: kv: 8 (over z_lo), pb: 8 (over x, z_hi), rep: 8 (over y, core).
Axes of the slice: x: 4, y: 4, z: 16 (z_hi: 2, z_lo: 8; z = z_hi * 8 + z_lo), core: 2. Of those that a mesh axis runs over, the one named last changes fastest.
Arguments:
- queries: bfloat16 [320, 64, 128], P('rep', ('kv', 'pb')), may hold values from -8 to 8
- prefix_cache: bfloat16 [8, 2, 4096, 128], P('kv', None, ('pb', 'rep')), may hold values from -8 to 8
- suffix_cache: bfloat16 [320, 8, 2, 512, 128], P('rep', 'kv', None, 'pb'), may hold values from -8 to 8
- suffix_lengths: int32 [320], P('rep'), may hold values from 1 to 512, as said below
- residual: float32 [320, 8192], P(('kv', 'pb'), 'rep'), may hold values from -120 to 120
- norm_gain: float32 [8192], P('rep'), may hold values from 0.1 to 1.9
- out_weight: bfloat16 [8192, 8192], P(('kv', 'pb'), 'rep'), may hold values from -0.5 to 0.5
- gate_weight: bfloat16 [8192, 29568], P('rep', ('kv', 'pb')), may hold values from -0.0625 to 0.0625
- up_weight: bfloat16 [8192, 29568], P('rep', ('kv', 'pb')), may hold values from -0.0625 to 0.0625
- down_weight: bfloat16 [29568, 8192], P(('kv', 'pb'), 'rep'), may hold values from -0.375 to 0.375
Outputs:
- context: bfloat16 [320, 64, 128], P('rep', ('kv', 'pb'))
- layer_out: float32 [320, 8192], P(('kv', 'pb'), 'rep')
Inputs may be any that keep to these rules, and one draw needn't show every extreme that they name: `suffix_lengths`: some row has exactly 512 live suffix positions.
All inputs are finite; a program needn't handle non-finite values.
Results may differ from a plain program's by a relative error of at most 0.024.
Values may be sent and summed in bfloat16 or wider, within the bound.
No kernel may reach another device: no remote copies, remote signals or barrier semaphores. Data moves between devices by JAX's collectives and lax.ppermute only.
A program may use at most 64 MiB of HBM per device.

v0:
```python
import jax
import jax.numpy as jnp
from jax import lax
from jax.sharding import PartitionSpec as P

D = 8192
HEAD_DIM = 128


lowest = -1e30
epsilon = 1e-06


def merge_parts(earlier_part, later_part):
    maxima_a, denoms_a, numers_a = earlier_part
    maxima_b, denoms_b, numers_b = later_part
    highest = jnp.maximum(maxima_a, maxima_b)
    first_factor = jnp.exp(maxima_a - highest)
    second_factor = jnp.exp(maxima_b - highest)
    return (
        highest,
        denoms_a * first_factor + denoms_b * second_factor,
        numers_a * first_factor[..., None] + numers_b * second_factor[..., None],
    )


def reduce_sources(partials, which_axis):
    maxima, denoms, numers = partials
    highest = jnp.max(maxima, axis=which_axis, keepdims=True)
    factor = jnp.exp(maxima - highest)
    return (
        jnp.squeeze(highest, which_axis),
        jnp.sum(denoms * factor, axis=which_axis),
        jnp.sum(numers * factor[..., None], axis=which_axis),
    )


def shared_part(query_rows, key_rows, value_rows):
    scores = jnp.einsum(
        "qd,td->qt", query_rows, key_rows, preferred_element_type=jnp.float32
    ) * HEAD_DIM ** (-0.5)
    highest = jnp.max(scores, axis=1)
    weights = jnp.exp(scores - highest[:, None])
    numers = jnp.dot(weights.astype(jnp.bfloat16), value_rows, preferred_element_type=jnp.float32)
    return (highest, jnp.sum(weights, axis=1), numers)


def suffix_part(group_queries, suffix_cache, suffix_lengths, offset):
    key_rows = suffix_cache[:, 0, 0]
    value_rows = suffix_cache[:, 0, 1]
    scores = jnp.einsum(
        "rgd,rsd->grs", group_queries, key_rows, preferred_element_type=jnp.float32
    ) * HEAD_DIM ** (-0.5)
    position = offset + lax.broadcasted_iota(jnp.int32, (key_rows.shape[0], key_rows.shape[1]), 1)
    is_live = (position < suffix_lengths[:, None])[None]
    scores = jnp.where(is_live, scores, lowest)
    highest = jnp.max(scores, axis=2)
    weights = jnp.where(is_live, jnp.exp(scores - highest[..., None]), 0.0)
    numers = jnp.einsum(
        "grs,rsd->grd", weights.astype(jnp.bfloat16), value_rows, preferred_element_type=jnp.float32
    )
    return (highest, jnp.sum(weights, axis=2), numers)


def per_device(
    queries,
    prefix_cache,
    suffix_cache,
    suffix_lengths,
    residual,
    norm_gain,
    out_weight,
    gate_weight,
    up_weight,
    down_weight,
):
    row_block = queries.shape[0]
    head_width = queries.shape[2]
    group_queries = lax.all_gather(queries, "pb", axis=1, tiled=True)
    offset = lax.axis_index("pb") * suffix_cache.shape[3]
    from_suffix = suffix_part(group_queries, suffix_cache, suffix_lengths, offset)
    own_queries = queries[:, 0, :]
    own_state = None
    start_state = (
        jnp.full((row_block,), lowest, jnp.float32),
        jnp.zeros((row_block,), jnp.float32),
        jnp.zeros((row_block, head_width), jnp.float32),
    )
    piece_rows = lax.all_gather(prefix_cache, ("pb", "rep"), axis=2, tiled=True)
    own_state = merge_parts(
        start_state, shared_part(own_queries, piece_rows[0, 0], piece_rows[0, 1])
    )
    arrived = reduce_sources(
        (
            lax.all_to_all(from_suffix[0], "pb", split_axis=0, concat_axis=0, tiled=True),
            lax.all_to_all(from_suffix[1], "pb", split_axis=0, concat_axis=0, tiled=True),
            lax.all_to_all(from_suffix[2], "pb", split_axis=0, concat_axis=0, tiled=True),
        ),
        0,
    )
    arrived = merge_parts(arrived, own_state)
    highest, denoms, numers = arrived
    context = (numers / denoms[:, None]).astype(jnp.bfloat16)
    all_context = lax.all_gather(context, "rep", axis=0, tiled=True)
    picked = all_context
    mixed = residual + lax.psum_scatter(
        jnp.dot(picked, out_weight, preferred_element_type=jnp.float32),
        ("kv", "pb"),
        scatter_dimension=0,
        tiled=True,
    )
    squares = lax.psum(jnp.sum(mixed * mixed, axis=1), "rep")
    normed = (mixed * lax.rsqrt(squares / D + epsilon)[:, None] * norm_gain).astype(jnp.bfloat16)
    piece_rows = lax.all_gather(normed, ("kv", "pb"), axis=0, tiled=True)
    partial_sums = jnp.concatenate(
        [
            jnp.dot(piece_rows, gate_weight, preferred_element_type=jnp.float32),
            jnp.dot(piece_rows, up_weight, preferred_element_type=jnp.float32),
        ],
        axis=1,
    )
    unit_count = gate_weight.shape[1]
    summed = lax.psum(partial_sums, "rep")
    hidden = (jax.nn.silu(summed[:, :unit_count]) * summed[:, unit_count:]).astype(jnp.bfloat16)
    picked = hidden
    layer_out = mixed + lax.psum_scatter(
        jnp.dot(picked, down_weight, preferred_element_type=jnp.float32),
        ("kv", "pb"),
        scatter_dimension=0,
        tiled=True,
    )
    return (context[:, None, :], layer_out)


def solution(mesh):
    in_specs = (
        P("rep", ("kv", "pb"), None),
        P("kv", None, ("pb", "rep"), None),
        P("rep", "kv", None, "pb", None),
        P("rep"),
        P(("kv", "pb"), "rep"),
        P("rep"),
        P(("kv", "pb"), "rep"),
        P("rep", ("kv", "pb")),
        P("rep", ("kv", "pb")),
        P(("kv", "pb"), "rep"),
    )
    out_specs = (P("rep", ("kv", "pb"), None), P(("kv", "pb"), "rep"))
    return jax.shard_map(
        per_device, mesh=mesh, in_specs=in_specs, out_specs=out_specs, check_vma=False
    )
```

profile of v0, /device:TPU:8, one launch (start us, length us, event | category | flops | bytes accessed | tf_op | source)
XLA Modules:
  0.0 1070.3 jit_solution(5785153689188876042)
XLA Ops:
  7.2 0.0 copy-start
  7.2 0.0 copy-start.3
  7.2 0.0 all-gather.3.cloned.1.call-start
  7.2 0.7 all-gather.3.cloned.1.call-update
  7.9 66.6 %all_gather.12 = bf16[40,8,128]{2,0,1:T(8,128)(2,1)S(1)} all-gather(bf16[40,1,128]{2,0,1:T(8,128)(2,1)} %param.10), channel_id=1, replica_groups=mesh['kv'=8,'pb'=8,'rep'=8] {'pb'}, dimensions={1}, use_global_device_ids=true | all-gather | bytes 92160 | tf_op jit(solution)/shard_map/all_gather | solution.py:79
  74.5 0.7 broadcast_compare_fusion
  75.2 1.6 fusion.35
  76.8 0.0 copy-start.5
  76.9 0.7 copy.27
  77.5 14.1 %all-to-all-start.1 = ((f32[8,1,40]{2,1,0:T(1,128)}), f32[8,1,40]{2,1,0:T(1,128)S(1)}, u32[]{:S(2)}, u32[]{:S(2)}) async-start(f32[8,1,40]{2,1,0:T(1,128)} %copy.27), calls=%async_computation.1 | async-start | bytes 8192 | tf_op jit(solution)/shard_map/all_to_all | solution.py:95
  91.7 0.2 fusion.19
  91.9 0.7 copy.28
  92.5 14.0 %all-to-all-done.1 = f32[8,1,40]{2,1,0:T(1,128)S(1)} async-done(((f32[8,1,40]{2,1,0:T(1,128)}), f32[8,1,40]{2,1,0:T(1,128)S(1)}, u32[]{:S(2)}, u32[]{:S(2)}) %all-to-all-start.1) | async-done | bytes 1312 | tf_op jit(solution)/shard_map/all_to_all | solution.py:95
  106.5 3.3 all-to-all-start.2
  109.8 0.0 copy-done.3
  109.8 0.3 convolution_bitcast_fusion
  110.2 0.7 copy.26
  110.9 13.6 %all-to-all-done.2 = f32[8,1,40]{2,1,0:T(1,128)S(1)} async-done(((f32[8,1,40]{2,1,0:T(1,128)}), f32[8,1,40]{2,1,0:T(1,128)S(1)}, u32[]{:S(2)}, u32[]{:S(2)}) %all-to-all-start.2) | async-done | bytes 1312 | tf_op jit(solution)/shard_map/all_to_all | solution.py:96
  124.5 3.4 all-to-all-start
  127.9 0.0 all-reduce.8.cloned.1.call-start
  128.0 16.4 %all-to-all-done = f32[8,40,128]{2,1,0:T(8,128)S(1)} async-done(((f32[8,40,128]{2,1,0:T(8,128)}), f32[8,40,128]{2,1,0:T(8,128)S(1)}, u32[]{:S(2)}, u32[]{:S(2)}) %all-to-all-start) | async-done | bytes 163872 | tf_op jit(solution)/shard_map/all_to_all | solution.py:97
  144.5 0.1 multiply_reduce_fusion
  144.6 0.0 all-gather.3.cloned.1.call-done
  144.6 0.0 copy-done.5
  144.6 0.0 copy-start.1
  144.6 2.2 fusion.34
  146.8 0.0 copy-start.4
  146.8 0.3 fusion.12
  147.1 0.0 copy-done.1
  147.1 0.4 fusion.6
  147.5 0.0 copy-start.6
  147.5 12.1 %all_gather.14 = bf16[320,128]{1,0:T(8,128)(2,1)S(1)} all-gather(bf16[40,128]{1,0:T(8,128)(2,1)S(1)} %fusion.6), channel_id=1, replica_groups=mesh['kv'=8,'pb'=8,'rep'=8] {'rep'}, dimensions={0}, use_global_device_ids=true | all-gather | bytes 92160 | tf_op jit(solution)/shard_map/all_gather | solution.py:104
  159.6 0.0 copy-done.4
  159.6 0.0 copy-start.7
  159.6 0.0 copy-start.8
  159.6 1.4 fusion.36
  161.0 0.0 all-reduce.8.cloned.1.call-update
  161.0 0.0 copy-done.6
  161.0 0.0 all-reduce.6.cloned.1.call-start
  161.1 1.3 dynamic-slice
  163.0 269.7 %all-reduce.8.cloned.1.call-done = f32[320,1024]{1,0:T(8,128)} async-done(((f32[320,1024]{1,0:T(8,128)}), f32[320,1024]{1,0:T(8,128)}) %all-reduce.8.cloned.1.call-update) | async-done | bytes 1310736
  432.7 0.0 copy-done.7
  432.7 1.0 multiply_reduce_fusion.1
  433.7 10.0 psum.14
  443.7 0.0 copy-done.8
  443.7 0.1 fusion.26
  443.8 260.8 %all-gather = bf16[64,5,1024]{2,1,0:T(8,128)(2,1)S(1)} all-gather(bf16[1,5,1024]{2,1,0:T(8,128)(2,1)S(1)} %fusion.26), channel_id=1, replica_groups=mesh['kv'=8,'pb'=8,'rep'=8] {'kv','pb'}, dimensions={0}, use_global_device_ids=true | all-gather | bytes 665600 | tf_op jit(solution)/shard_map/all_gather | solution.py:114
  704.6 0.3 reshape.91
  704.9 0.0 copy-start.2
  704.9 1.8 fusion.38
  706.7 0.0 copy-done.2
  706.7 0.5 fusion.37
  707.3 1.4 pad_maximum_fusion
  708.6 0.0 all-reduce.6.cloned.1.call-update
  708.7 0.0 all-reduce.10.cloned.1.call-start
  708.7 73.5 %all-reduce.6.cloned.1.call-done = f32[320,924]{1,0:T(8,128)} async-done(((f32[320,924]{1,0:T(8,128)}), f32[320,924]{1,0:T(8,128)}) %all-reduce.6.cloned.1.call-update) | async-done | bytes 1182736 | tf_op jit(solution)/shard_map/psum | solution.py:123
  782.2 0.0 copy-done
  782.2 3.0 fusion.15
  785.2 0.0 all-reduce.10.cloned.1.call-update
  785.2 277.1 %all-reduce.10.cloned.1.call-done = f32[320,1024]{1,0:T(8,128)} async-done(((f32[320,1024]{1,0:T(8,128)}), f32[320,1024]{1,0:T(8,128)}) %all-reduce.10.cloned.1.call-update) | async-done | bytes 1310736
  1062.3 1.5 dynamic-slice_add_fusion
  (5 shorter events, 0.1 us)
Async XLA Ops:
  7.2 775.0 %copy-start = (bf16[462,1024]{1,0:T(8,128)(2,1)S(1)}, bf16[462,1024]{1,0:T(8,128)(2,1)}, u32[]{:S(2)}) copy-start(bf16[462,1024]{1,0:T(8,128)(2,1)} %param.19) | copy-start | bytes 2838532
  7.2 102.6 %copy-start.3 = (bf16[40,1,2,64,128]{4,3,2,1,0:T(8,128)(2,1)S(1)}, bf16[40,1,2,64,128]{4,3,2,1,0:T(8,128)(2,1)}, u32[]{:S(2)}) copy-start(bf16[40,1,2,64,128]{4,3,2,1,0:T(8,128)(2,1)} %param.12) | copy-start | bytes 3932164
  7.2 137.4 %all-gather.3.cloned.1.call-start = ((), (), s32[]{:S(2)}) async-start(), calls=%async_computation.3 | async-start | bytes 2129920 | tf_op jit(solution)/shard_map/all_gather | solution.py:89
  76.8 67.8 %copy-start.5 = (bf16[40,1,128]{2,0,1:T(8,128)(2,1)S(1)}, bf16[40,1,128]{2,0,1:T(8,128)(2,1)}, u32[]{:S(2)}) copy-start(bf16[40,1,128]{2,0,1:T(8,128)(2,1)} %param.10) | copy-start | bytes 30724
  77.5 29.0 %all-to-all-start.1 = ((f32[8,1,40]{2,1,0:T(1,128)}), f32[8,1,40]{2,1,0:T(1,128)S(1)}, u32[]{:S(2)}, u32[]{:S(2)}) async-start(f32[8,1,40]{2,1,0:T(1,128)} %copy.27), calls=%async_computation.1 | async-start | bytes 8192 | tf_op jit(solution)/shard_map/all_to_all | solution.py:95
  106.5 18.0 %all-to-all-start.2 = ((f32[8,1,40]{2,1,0:T(1,128)}), f32[8,1,40]{2,1,0:T(1,128)S(1)}, u32[]{:S(2)}, u32[]{:S(2)}) async-start(f32[8,1,40]{2,1,0:T(1,128)} %copy.28), calls=%async_computation.2 | async-start | bytes 8192 | tf_op jit(solution)/shard_map/all_to_all | solution.py:96
  124.5 19.9 %all-to-all-start = ((f32[8,40,128]{2,1,0:T(8,128)}), f32[8,40,128]{2,1,0:T(8,128)S(1)}, u32[]{:S(2)}, u32[]{:S(2)}) async-start(f32[8,40,128]{2,1,0:T(8,128)} %copy.26), calls=%async_computation | async-start | bytes 327680 | tf_op jit(solution)/shard_map/all_to_all | solution.py:97
  127.9 304.8 %all-reduce.8.cloned.1.call-start = ((), (), s32[]{:S(2)}) async-start(), calls=%async_computation.5 | async-start | bytes 2621440
  144.6 2.5 copy-start.1
  146.8 12.8 %copy-start.4 = (bf16[128,1024]{1,0:T(8,128)(2,1)S(1)}, bf16[128,1024]{1,0:T(8,128)(2,1)}, u32[]{:S(2)}) copy-start(bf16[128,1024]{1,0:T(8,128)(2,1)} %param.16) | copy-start | bytes 786436
  147.5 13.5 %copy-start.6 = (bf16[40,128]{1,0:T(8,128)(2,1)}, bf16[40,128]{1,0:T(8,128)(2,1)S(1)}, u32[]{:S(2)}) copy-start(bf16[40,128]{1,0:T(8,128)(2,1)S(1)} %fusion.6) | copy-start | bytes 30724
  159.6 273.1 %copy-start.7 = (f32[5,1024]{1,0:T(8,128)S(1)}, f32[5,1024]{1,0:T(8,128)}, u32[]{:S(2)}) copy-start(f32[5,1024]{1,0:T(8,128)} %param.14) | copy-start | bytes 61444
  159.6 284.1 %copy-start.8 = (f32[1024]{0:T(1024)S(1)}, f32[1024]{0:T(1024)}, u32[]{:S(2)}) copy-start(f32[1024]{0:T(1024)} %param.15) | copy-start | bytes 12292
  161.0 621.2 %all-reduce.6.cloned.1.call-start = ((), (), s32[]{:S(2)}) async-start(), calls=%async_computation.4 | async-start | bytes 2621440 | tf_op jit(solution)/shard_map/psum | solution.py:123
  704.9 1.8 copy-start.2
  708.7 353.6 %all-reduce.10.cloned.1.call-start = ((), (), s32[]{:S(2)}) async-start(), calls=%async_computation.6 | async-start | bytes 2621440
Sparse Core Ops, SparseCore 0:
  12.6 117.7 all-gather.2
  161.1 271.5 all-reduce.7
  708.8 73.3 all-reduce.5
  785.4 276.8 all-reduce.9
where the time goes:
time: 1070 us
  waiting for transfers between devices  665 us (62%)
  blocking collectives  349 us (33%)
  starting transfers between devices  21 us (2%)
  between operations  14.6 us (1%)
  matrix products  11.2 us (1%)
    unnamed x6, waiting for transfers between devices  548 us
    all_gather x1, blocking collectives, per_device(): piece_rows = lax.all_gather(normed, ('kv', 'pb'), axis=0, tiled=True)  261 us
    psum x1, waiting for transfers between devices, per_device(): summed = lax.psum(partial_sums, 'rep')  73.5 us
    all_gather x1, blocking collectives, per_device(): group_queries = lax.all_gather(queries, 'pb', axis=1, tiled=True)  66.6 us
  transfers between devices with their start and end apart: 7, of which 6 were waited for; matrix products, arithmetic and copies ran while one was open for 1% of the time, Pallas kernels for 0%

commit v1 on v0

v1 whole, which is shorter than its diff:
```python
import jax
import jax.numpy as jnp
from jax import lax
from jax.sharding import PartitionSpec as P

D = 8192
HEAD_DIM = 128
X = 4
ZH = 2

lowest = -1e30
epsilon = 1e-06
f32 = jnp.float32
bf16 = jnp.bfloat16

x_groups = [[x * ZH + zh for x in range(X)] for zh in range(ZH)]
z_groups = [[kv * 8 + x * ZH + zh for kv in range(8) for zh in range(ZH)] for x in range(X)]


def exchange(blocks, axes, groups=None):
    return lax.all_to_all(blocks, axes, 0, 0, axis_index_groups=groups, tiled=True)


def spread(block, count, axes, groups=None):
    return exchange(jnp.broadcast_to(block[None], (count,) + block.shape), axes, groups)


def split_float(value):
    high = lax.reduce_precision(value, 8, 7)
    rest = value - high
    middle = lax.reduce_precision(rest, 8, 7)
    return high.astype(bf16), middle.astype(bf16), (rest - middle).astype(bf16)


def local_attention(queries, prefix, suffix, lengths, offset):
    scale = HEAD_DIM ** (-0.5)
    heads, rows, width = queries.shape
    shared = jnp.einsum("grd,td->grt", queries, prefix[0], preferred_element_type=f32) * scale
    own = jnp.einsum("grd,rsd->grs", queries, suffix[:, 0], preferred_element_type=f32) * scale
    position = offset + lax.broadcasted_iota(jnp.int32, (rows, suffix.shape[2]), 1)
    is_live = (position < lengths[:, None])[None]
    own = jnp.where(is_live, own, lowest)
    highest = jnp.maximum(jnp.max(shared, axis=2), jnp.max(own, axis=2))
    shared_weights = jnp.exp(shared - highest[..., None])
    own_weights = jnp.where(is_live, jnp.exp(own - highest[..., None]), 0.0)
    denoms = jnp.sum(shared_weights, axis=2) + jnp.sum(own_weights, axis=2)
    numers = jnp.einsum(
        "grt,td->grd", shared_weights.astype(bf16), prefix[1], preferred_element_type=f32
    ) + jnp.einsum(
        "grs,rsd->grd", own_weights.astype(bf16), suffix[:, 1], preferred_element_type=f32
    )
    return highest, denoms, numers


def sum_over_owners(partial):
    rows, n = partial.shape
    over_x = exchange(partial.astype(bf16).reshape(X, rows // X, n), "pb", x_groups)
    over_x = jnp.sum(over_x.astype(f32), axis=0)
    over_z = exchange(over_x.astype(bf16).reshape(16, rows // 64, n), ("kv", "pb"), z_groups)
    return jnp.sum(over_z.astype(f32), axis=0)


def per_device(
    queries,
    prefix_cache,
    suffix_cache,
    suffix_lengths,
    residual,
    norm_gain,
    out_weight,
    gate_weight,
    up_weight,
    down_weight,
):
    rows, _, width = queries.shape
    units = gate_weight.shape[1]
    prefix = lax.all_gather(prefix_cache[0], "rep", axis=1, tiled=True)
    group_queries = spread(queries[:, 0, :], 8, "pb")
    offset = lax.axis_index("pb") * suffix_cache.shape[3]
    highest, denoms, numers = local_attention(
        group_queries, prefix, suffix_cache[:, 0], suffix_lengths, offset
    )
    logs = highest + jnp.log(denoms)
    stats = jnp.pad(jnp.stack(split_float(logs), axis=1), ((0, 0), (0, 5), (0, width - rows)))
    parts = jnp.concatenate([(numers / denoms[..., None]).astype(bf16), stats], axis=1)
    parts = exchange(parts, "pb").astype(f32)
    logs = jnp.sum(parts[:, rows : rows + 3, :rows], axis=1)
    factor = jnp.exp(logs - jnp.max(logs, axis=0))
    factor = factor / jnp.sum(factor, axis=0)
    context = jnp.sum(parts[:, :rows] * factor[..., None], axis=0).astype(bf16)

    all_context = spread(context, 8, "rep").reshape(8, X, rows // X, width)
    all_context = all_context.transpose(1, 0, 2, 3).reshape(8 * rows, width)
    attended = jnp.dot(all_context, out_weight, preferred_element_type=f32)
    mixed = residual + sum_over_owners(attended)

    squares = jnp.sum(mixed * mixed, axis=1, keepdims=True)
    squares = jnp.concatenate(split_float(squares), axis=1)
    sent = jnp.concatenate(
        [(mixed * norm_gain).astype(bf16), jnp.pad(squares, ((0, 0), (0, 125)))], axis=1
    )
    sent = spread(sent, 16, ("kv", "pb"), z_groups).reshape(2 * rows, -1)
    sent = spread(sent, X, "pb", x_groups).reshape(8 * rows, -1)
    scaled, squares = sent[:, : mixed.shape[1]], sent[:, mixed.shape[1] : mixed.shape[1] + 3]
    gates = jnp.dot(scaled, gate_weight, preferred_element_type=f32).astype(bf16)
    ups = jnp.dot(scaled, up_weight, preferred_element_type=f32).astype(bf16)
    partial = jnp.concatenate(
        [
            jnp.pad(jnp.concatenate([gates, squares], axis=1), ((0, 0), (0, 512 - units - 3))),
            jnp.pad(ups, ((0, 0), (0, 512 - units))),
        ],
        axis=1,
    )
    summed = jnp.sum(exchange(partial.reshape(8, rows, 1024), "rep").astype(f32), axis=0)
    inverse = lax.rsqrt(jnp.sum(summed[:, units : units + 3], axis=1, keepdims=True) / D + epsilon)
    gates = summed[:, :units] * inverse
    ups = summed[:, 512 : 512 + units] * inverse
    hidden = (jax.nn.silu(gates) * ups).astype(bf16)
    hidden = spread(hidden, 8, "rep").reshape(8 * rows, units)
    layer_out = mixed + sum_over_owners(jnp.dot(hidden, down_weight, preferred_element_type=f32))
    return (context[:, None, :], layer_out)


def solution(mesh):
    in_specs = (
        P("rep", ("kv", "pb"), None),
        P("kv", None, ("pb", "rep"), None),
        P("rep", "kv", None, "pb", None),
        P("rep"),
        P(("kv", "pb"), "rep"),
        P("rep"),
        P(("kv", "pb"), "rep"),
        P("rep", ("kv", "pb")),
        P("rep", ("kv", "pb")),
        P(("kv", "pb"), "rep"),
    )
    out_specs = (P("rep", ("kv", "pb"), None), P(("kv", "pb"), "rep"))
    return jax.shard_map(
        per_device, mesh=mesh, in_specs=in_specs, out_specs=out_specs, check_vma=False
    )
```

time: 1070 us -> 220 us (0.21)
  the two profiles are of different devices: /device:TPU:8 before, /device:TPU:32 now
where the time goes in v1:
time: 220 us; the launch traced here: 219 us
  blocking collectives  191 us (87%)
  starting transfers between devices  16.7 us (8%)
  local copies, waits for them, and re-layouts  4.27 us (2%)
  matrix products  3.43 us (2%)
  other arithmetic  2.49 us (1%)
    all_to_all x10, blocking collectives, exchange(): lax.all_to_all(blocks, axes, 0, 0, axis_index_groups=groups, tiled=True)  178 us
    all_to_all x1, starting transfers between devices, exchange(): lax.all_to_all(blocks, axes, 0, 0, axis_index_groups=groups, tiled=True)  16.7 us
    all_gather x1, blocking collectives, per_device(): prefix = lax.all_gather(prefix_cache[0], 'rep', axis=1, tiled=True)  13.6 us
  transfers between devices with their start and end apart: 1, of which 0 were waited for; matrix products, arithmetic and copies ran while one was open for 1% of the time, Pallas kernels for 0%

profile of v1, /device:TPU:32, one launch (start us, length us, event | category | flops | bytes accessed | tf_op | source)
XLA Modules:
  0.0 219.0 jit_solution(12359283447168659210)
XLA Ops:
  0.6 0.0 copy-start
  0.6 1.4 broadcast_in_dim.35
  2.1 16.7 %all-to-all-start = ((bf16[8,40,128]{2,1,0:T(8,128)(2,1)}), bf16[8,40,128]{2,1,0:T(8,128)(2,1)S(1)}, u32[]{:S(2)}, u32[]{:S(2)}) async-start(bf16[8,40,128]{2,1,0:T(8,128)(2,1)} %broadcast_in_dim.35), calls=%async_computation | async-start | bytes 163840 | tf_op jit(solution)/shard_map/all_to_all | solution.py:21
  18.7 13.6 %all-gather = bf16[1,2,512,128]{3,2,1,0:T(8,128)(2,1)S(1)} all-gather(bf16[1,2,64,128]{3,2,1,0:T(8,128)(2,1)} %param.11), channel_id=2, replica_groups=mesh['kv'=8,'pb'=8,'rep'=8] {'rep'}, dimensions={2}, use_global_device_ids=true | all-gather | bytes 294912 | tf_op jit(solution)/shard_map/all_gather | solution.py:77
  32.3 0.0 copy-start.5
  32.3 1.4 copy.72
  33.7 0.0 copy-done.5
  33.7 0.1 broadcast_compare_fusion
  33.8 0.0 all-to-all-done
  33.9 0.5 fusion.36
  34.4 0.1 copy.54
  34.4 0.4 fusion.35
  34.8 0.1 copy.55
  34.9 0.3 fusion.8
  35.2 0.2 fusion.18
  35.5 0.2 fusion.9
  35.7 0.1 copy.57
  35.8 0.0 copy-start.1
  35.8 0.3 fusion.4
  36.2 32.5 %all_to_all.55 = bf16[8,48,128]{2,1,0:T(8,128)(2,1)S(1)} all-to-all(bf16[8,48,128]{2,1,0:T(8,128)(2,1)S(1)} %fusion.20), channel_id=1, replica_groups=mesh['kv'=8,'pb'=8,'rep'=8] {'pb'}, dimensions={0} | all-to-all | bytes 196608 | tf_op jit(solution)/shard_map/all_to_all | solution.py:21
  68.8 0.1 fusion.17
  68.9 0.0 copy-start.2
  68.9 9.3 %all_to_all.56 = bf16[8,40,128]{2,1,0:T(8,128)(2,1)S(1)} all-to-all(bf16[8,40,128]{2,1,0:T(8,128)(2,1)S(1)} %broadcast_in_dim.70), channel_id=1, replica_groups=mesh['kv'=8,'pb'=8,'rep'=8] {'rep'}, dimensions={0} | all-to-all | bytes 163840 | tf_op jit(solution)/shard_map/all_to_all | solution.py:21
  78.3 0.0 copy-done.1
  78.3 0.3 convolution_convert_fusion
  78.6 13.4 %all_to_all.57 = bf16[4,80,1024]{2,1,0:T(8,128)(2,1)S(1)} all-to-all(bf16[4,80,1024]{2,1,0:T(8,128)(2,1)S(1)} %bitcast.61), channel_id=1, replica_groups={{0,16,32,48},{8,24,40,56},{1,17,33,49},{9,25,41,57},{2,18,34,50},{10,26..., dimensions={0} | all-to-all | bytes 1310720 | tf_op jit(solution)/shard_map/all_to_all | solution.py:21
  92.1 0.0 copy-done.2
  92.1 0.0 copy-start.3
  92.1 0.0 copy-start.4
  92.1 0.1 reduce_sum.121
  92.2 0.1 reshape.245
  92.3 22.9 %all_to_all.58 = bf16[16,5,1024]{2,1,0:T(8,128)(2,1)S(1)} all-to-all(bf16[16,5,1024]{2,1,0:T(8,128)(2,1)S(1)} %reshape.245), channel_id=1, replica_groups={{0,8,64,72,128,136,192,200,256,264,320,328,384,392,448,456},{16,24,80,8..., dimensions={0} | all-to-all | bytes 327680 | tf_op jit(solution)/shard_map/all_to_all | solution.py:21
  115.1 0.1 convert_reduce_fusion.2
  115.2 0.0 copy-done.3
  115.2 0.0 copy-done.4
  115.2 0.1 multiply_reduce_fusion
  115.4 0.1 copy.65
  115.5 24.6 %all_to_all.59 = bf16[16,5,1152]{2,1,0:T(8,128)(2,1)S(1)} all-to-all(bf16[16,5,1152]{2,1,0:T(8,128)(2,1)S(1)} %broadcast_in_dim.71), channel_id=1, replica_groups={{0,8,64,72,128,136,192,200,256,264,320,328,384,392,448,456},{16,24,80,8..., dimensions={0} | all-to-all | bytes 368640 | tf_op jit(solution)/shard_map/all_to_all | solution.py:21
  140.1 0.1 broadcast_in_dim.72
  140.2 0.0 copy-start.6
  140.2 0.1 broadcast_in_dim.73
  140.3 11.8 %all_to_all.60 = bf16[4,80,1152]{2,1,0:T(8,128)(2,1)S(1)} all-to-all(bf16[4,80,1152]{2,1,0:T(8,128)(2,1)S(1)} %broadcast_in_dim.73), channel_id=1, replica_groups={{0,16,32,48},{8,24,40,56},{1,17,33,49},{9,25,41,57},{2,18,34,50},{10,26..., dimensions={0} | all-to-all | bytes 1474560 | tf_op jit(solution)/shard_map/all_to_all | solution.py:21
  152.0 0.0 copy-start.7
  152.0 0.0 copy-done.6
  152.0 0.5 convolution_convert_fusion.2
  152.6 0.6 copy-done.7
  153.2 0.5 convolution_convert_fusion.3
  153.7 0.1 fusion.14
  153.8 0.1 fusion.5
  153.9 14.2 %all_to_all.61 = bf16[8,40,1024]{2,1,0:T(8,128)(2,1)S(1)} all-to-all(bf16[8,40,1024]{2,1,0:T(8,128)(2,1)S(1)} %bitcast.60), channel_id=1, replica_groups=mesh['kv'=8,'pb'=8,'rep'=8] {'rep'}, dimensions={0} | all-to-all | bytes 1310720 | tf_op jit(solution)/shard_map/all_to_all | solution.py:21
  168.1 0.1 convert_reduce_fusion
  168.2 0.2 slice_reduce_fusion
  168.4 0.1 fusion.23
  168.6 10.6 %all_to_all.62 = bf16[8,40,462]{2,1,0:T(8,128)(2,1)S(1)} all-to-all(bf16[8,40,462]{2,1,0:T(8,128)(2,1)S(1)} %broadcast_in_dim.74), channel_id=1, replica_groups=mesh['kv'=8,'pb'=8,'rep'=8] {'rep'}, dimensions={0} | all-to-all | bytes 591360 | tf_op jit(solution)/shard_map/all_to_all | solution.py:21
  179.2 0.0 copy-done
  179.2 0.5 convolution_convert_fusion.1
  179.7 13.5 %all_to_all.63 = bf16[4,80,1024]{2,1,0:T(8,128)(2,1)S(1)} all-to-all(bf16[4,80,1024]{2,1,0:T(8,128)(2,1)S(1)} %bitcast.62), channel_id=1, replica_groups={{0,16,32,48},{8,24,40,56},{1,17,33,49},{9,25,41,57},{2,18,34,50},{10,26..., dimensions={0} | all-to-all | bytes 1310720 | tf_op jit(solution)/shard_map/all_to_all | solution.py:21
  193.2 0.1 reduce_sum.127
  193.3 0.1 reshape.250
  193.4 25.0 %all_to_all.64 = bf16[16,5,1024]{2,1,0:T(8,128)(2,1)S(1)} all-to-all(bf16[16,5,1024]{2,1,0:T(8,128)(2,1)S(1)} %reshape.250), channel_id=1, replica_groups={{0,8,64,72,128,136,192,200,256,264,320,328,384,392,448,456},{16,24,80,8..., dimensions={0} | all-to-all | bytes 327680 | tf_op jit(solution)/shard_map/all_to_all | solution.py:21
  218.4 0.1 convert_reduce_fusion.1
  218.4 0.6 add.93
  (24 shorter events, 0.3 us)
Async XLA Ops:
  0.6 178.6 %copy-start = (bf16[462,1024]{1,0:T(8,128)(2,1)S(1)}, bf16[462,1024]{1,0:T(8,128)(2,1)}, u32[]{:S(2)}) copy-start(bf16[462,1024]{1,0:T(8,128)(2,1)} %param.19) | copy-start | bytes 2838532
  2.1 31.8 %all-to-all-start = ((bf16[8,40,128]{2,1,0:T(8,128)(2,1)}), bf16[8,40,128]{2,1,0:T(8,128)(2,1)S(1)}, u32[]{:S(2)}, u32[]{:S(2)}) async-start(bf16[8,40,128]{2,1,0:T(8,128)(2,1)} %broadcast_in_dim.35), calls=%async_computation | async-start | bytes 163840 | tf_op jit(solution)/shard_map/all_to_all | solution.py:21
  32.3 1.5 copy-start.5
  35.8 42.5 %copy-start.1 = (bf16[128,1024]{1,0:T(8,128)(2,1)S(1)}, bf16[128,1024]{1,0:T(8,128)(2,1)}, u32[]{:S(2)}) copy-start(bf16[128,1024]{1,0:T(8,128)(2,1)} %param.16) | copy-start | bytes 786436
  68.9 23.2 %copy-start.2 = (bf16[40,128]{1,0:T(8,128)(2,1)}, bf16[40,128]{1,0:T(8,128)(2,1)S(1)}, u32[]{:S(2)}) copy-start(bf16[40,128]{1,0:T(8,128)(2,1)S(1)} %fusion.17) | copy-start | bytes 30724
  92.1 23.1 %copy-start.3 = (f32[5,1024]{1,0:T(8,128)S(1)}, f32[5,1024]{1,0:T(8,128)}, u32[]{:S(2)}) copy-start(f32[5,1024]{1,0:T(8,128)} %param.14) | copy-start | bytes 61444
  92.1 23.1 %copy-start.4 = (f32[1024]{0:T(1024)S(1)}, f32[1024]{0:T(1024)}, u32[]{:S(2)}) copy-start(f32[1024]{0:T(1024)} %param.15) | copy-start | bytes 12292
  140.2 11.8 %copy-start.6 = (bf16[1024,462]{0,1:T(8,128)(2,1)S(1)}, bf16[1024,462]{0,1:T(8,128)(2,1)}, u32[]{:S(2)}) copy-start(bf16[1024,462]{0,1:T(8,128)(2,1)} %param.18) | copy-start | bytes 2838532
  152.0 1.2 copy-start.7

commit v2 on v1

v2 whole, which is shorter than its diff:
```python
import functools

import jax
import jax.numpy as jnp
from jax import lax
from jax.experimental import pallas as pl
from jax.experimental.pallas import tpu as pltpu
from jax.sharding import PartitionSpec as P

D = 8192
HEAD_DIM = 128
X = 4
ZH = 2
Z = 16
LANES = 128

lowest = -1e30
epsilon = 1e-06
f32 = jnp.float32
bf16 = jnp.bfloat16

x_groups = [[x * ZH + zh for x in range(X)] for zh in range(ZH)]
z_groups = [[kv * 8 + x * ZH + zh for zh in range(ZH) for kv in range(8)] for x in range(X)]


def exchange(blocks, axes, groups=None):
    return lax.all_to_all(blocks, axes, 0, 0, axis_index_groups=groups, tiled=True)


def spread(block, count, axes, groups=None):
    return exchange(jnp.broadcast_to(block[None], (count,) + block.shape), axes, groups)


def split_float(value):
    high = lax.reduce_precision(value, 8, 7)
    rest = value - high
    middle = lax.reduce_precision(rest, 8, 7)
    return high.astype(bf16), middle.astype(bf16), (rest - middle).astype(bf16)


def local_attention(queries, prefix, suffix, lengths, offset):
    scale = HEAD_DIM ** (-0.5)
    heads, rows, width = queries.shape
    shared = jnp.einsum("grd,td->grt", queries, prefix[0], preferred_element_type=f32) * scale
    own = jnp.einsum("grd,rsd->grs", queries, suffix[:, 0], preferred_element_type=f32) * scale
    position = offset + lax.broadcasted_iota(jnp.int32, (rows, suffix.shape[2]), 1)
    is_live = (position < lengths[:, None])[None]
    own = jnp.where(is_live, own, lowest)
    highest = jnp.maximum(jnp.max(shared, axis=2), jnp.max(own, axis=2))
    shared_weights = jnp.exp(shared - highest[..., None])
    own_weights = jnp.where(is_live, jnp.exp(own - highest[..., None]), 0.0)
    denoms = jnp.sum(shared_weights, axis=2) + jnp.sum(own_weights, axis=2)
    numers = jnp.einsum(
        "grt,td->grd", shared_weights.astype(bf16), prefix[1], preferred_element_type=f32
    ) + jnp.einsum(
        "grs,rsd->grd", own_weights.astype(bf16), suffix[:, 1], preferred_element_type=f32
    )
    return highest, denoms, numers


def gate_up_body(rows_ref, inverse_gain_ref, gate_ref, up_ref, out_ref):
    units = gate_ref.shape[0]
    contract = (((1,), (1,)), ((), ()))
    rows = rows_ref[...]
    gates = lax.dot_general(rows, gate_ref[...], contract, preferred_element_type=f32)
    out_ref[:, :units] = gates.astype(bf16)
    ups = lax.dot_general(rows, up_ref[...], contract, preferred_element_type=f32)
    out_ref[:, 512 : 512 + units] = ups.astype(bf16)
    mixed = rows.astype(f32) * inverse_gain_ref[...]
    squares = jnp.sum(mixed * mixed, axis=1, keepdims=True)
    high = squares.astype(bf16)
    squares = squares - high.astype(f32)
    middle = squares.astype(bf16)
    low = (squares - middle.astype(f32)).astype(bf16)
    for i, value in enumerate((high, middle, low)):
        out_ref[:, units + i : units + i + 1] = value


def gate_up(rows, inverse_gain, gates, ups):
    return pl.pallas_call(
        gate_up_body,
        in_specs=[pl.BlockSpec(memory_space=pltpu.VMEM)] * 4,
        out_specs=pl.BlockSpec(memory_space=pltpu.VMEM),
        out_shape=jax.ShapeDtypeStruct((rows.shape[0], 1024), bf16),
        compiler_params=pltpu.CompilerParams(vmem_limit_bytes=24 * 2**20),
    )(rows, inverse_gain, gates, ups)


def per_device(
    queries,
    prefix_cache,
    suffix_cache,
    suffix_lengths,
    residual,
    norm_gain,
    out_weight,
    gate_weight,
    up_weight,
    down_weight,
):
    rows, _, width = queries.shape
    units = gate_weight.shape[1]
    part = rows // X
    own, columns = residual.shape
    z_at = lax.axis_index("pb") % ZH * 8 + lax.axis_index("kv")
    own_rows = lax.dynamic_update_slice(
        jnp.zeros((2 * rows, columns), f32), residual, (z_at * own, 0)
    )
    block_gain = lax.dynamic_slice(norm_gain, (z_at % 8 * LANES,), (LANES,))
    prefix = lax.all_gather(prefix_cache[0], "rep", axis=1, tiled=True)
    group_queries = spread(queries[:, 0, :], 8, "pb")
    offset = lax.axis_index("pb") * suffix_cache.shape[3]
    highest, denoms, numers = local_attention(
        group_queries, prefix, suffix_cache[:, 0], suffix_lengths, offset
    )

    logs = highest + jnp.log(denoms)
    stats = jnp.pad(jnp.stack(split_float(logs), axis=1), ((0, 0), (0, 5), (0, width - rows)))
    parts = (numers / denoms[..., None]).astype(bf16)
    parts = exchange(jnp.concatenate([parts, stats], axis=1), "pb").astype(f32)
    logs = jnp.sum(parts[:, rows : rows + 3, :rows], axis=1)
    factor = jnp.exp(logs - jnp.max(logs, axis=0))
    factor = factor / jnp.sum(factor, axis=0)
    context = jnp.sum(parts[:, :rows] * factor[..., None], axis=0).astype(bf16)
    all_context = spread(context, 8, "rep").reshape(8, X, ZH, part // ZH, width)
    all_context = all_context.transpose(1, 2, 0, 3, 4).reshape(8 * rows, width)
    attended = jnp.dot(all_context, out_weight, preferred_element_type=f32).astype(bf16)
    attended = exchange(attended.reshape(X, 2 * rows, columns), "pb", x_groups)
    attended = jnp.sum(attended.astype(f32), axis=0)
    blocks = (attended + own_rows).astype(bf16).reshape(2, rows, Z // 2, LANES)
    blocks = blocks.swapaxes(1, 2).reshape(Z, rows, LANES)
    block = jnp.sum(exchange(blocks, ("kv", "pb"), z_groups).astype(f32), axis=0)
    block = (block * block_gain).astype(bf16)
    sent = spread(block, Z, ("kv", "pb"), z_groups).reshape(-1, LANES)
    sent = spread(sent, X, "pb", x_groups)
    scaled = sent.reshape(2 * X, Z // 2, rows, LANES).swapaxes(1, 2)
    scaled = scaled.reshape(8 * rows, columns)
    partial = gate_up(scaled, 1.0 / norm_gain[None], gate_weight.T, up_weight.T)
    partial = exchange(partial.reshape(8, rows, 1024), "rep")
    summed = jnp.sum(partial.astype(f32), axis=0)
    inverse = lax.rsqrt(jnp.sum(summed[:, units : units + 3], axis=1, keepdims=True) / D + epsilon)
    gates = summed[:, :units] * inverse
    ups = summed[:, 512 : 512 + units] * inverse
    hidden = (jax.nn.silu(gates) * ups).astype(bf16)
    hidden = spread(hidden, 8, "rep").reshape(8 * rows, units)
    out = jnp.dot(hidden, down_weight, preferred_element_type=f32).astype(bf16)
    out = exchange(out.reshape(X, 2 * rows, columns), "pb", x_groups)
    out = jnp.sum(out.astype(f32), axis=0) + attended
    out = exchange(out.astype(bf16).reshape(Z, -1, LANES), ("kv", "pb"), z_groups)
    out = jnp.sum(out.astype(f32), axis=0).reshape(own, columns)
    return (context[:, None, :], residual + out)


def solution(mesh):
    in_specs = (
        P("rep", ("kv", "pb"), None),
        P("kv", None, ("pb", "rep"), None),
        P("rep", "kv", None, "pb", None),
        P("rep"),
        P(("kv", "pb"), "rep"),
        P("rep"),
        P(("kv", "pb"), "rep"),
        P("rep", ("kv", "pb")),
        P("rep", ("kv", "pb")),
        P(("kv", "pb"), "rep"),
    )
    out_specs = (P("rep", ("kv", "pb"), None), P(("kv", "pb"), "rep"))
    return jax.shard_map(
        per_device, mesh=mesh, in_specs=in_specs, out_specs=out_specs, check_vma=False
    )
```

time: 220 us -> 207 us (0.941)
  blocking collectives: 191 us -> 131 us
  waiting for transfers between devices: 0.04 us -> 33.8 us
  starting transfers between devices: 16.7 us -> 27.2 us
  local copies, waits for them, and re-layouts: 4.27 us -> 6.8 us
    all_to_all x10 -> x7, blocking collectives: 178 us -> 118 us  [exchange(): lax.all_to_all(blocks, axes, 0, 0, axis_index_groups=groups, tiled=True)]
    all_to_all x1 -> x4, waiting for transfers between devices: 0.04 us -> 33.8 us  [exchange(): lax.all_to_all(blocks, axes, 0, 0, axis_index_groups=groups, tiled=True)]
    all_to_all x1 -> x4, starting transfers between devices: 16.7 us -> 27.2 us  [exchange(): lax.all_to_all(blocks, axes, 0, 0, axis_index_groups=groups, tiled=True)]
  transfers between devices with their start and end apart: 1 -> 4, of which waited for: 0 -> 3; matrix products, arithmetic and copies ran while one was open for 1% -> 1% of each run, Pallas kernels for 0% -> 0%
where the time goes in v2:
time: 207 us; the launch traced here: 206 us
  blocking collectives  131 us (63%)
  waiting for transfers between devices  33.8 us (16%)
  starting transfers between devices  27.2 us (13%)
  local copies, waits for them, and re-layouts  6.8 us (3%)
  matrix products  3.21 us (2%)
  other arithmetic  2.14 us (1%)
    all_to_all x7, blocking collectives, exchange(): lax.all_to_all(blocks, axes, 0, 0, axis_index_groups=groups, tiled=True)  118 us
    all_to_all x4, waiting for transfers between devices, exchange(): lax.all_to_all(blocks, axes, 0, 0, axis_index_groups=groups, tiled=True)  33.8 us
    all_to_all x4, starting transfers between devices, exchange(): lax.all_to_all(blocks, axes, 0, 0, axis_index_groups=groups, tiled=True)  27.2 us
    all_gather x1, blocking collectives, per_device(): prefix = lax.all_gather(prefix_cache[0], 'rep', axis=1, tiled=True)  13.6 us
  transfers between devices with their start and end apart: 4, of which 3 were waited for; matrix products, arithmetic and copies ran while one was open for 1% of the time, Pallas kernels for 0%

profile of v2, /device:TPU:32, one launch (start us, length us, event | category | flops | bytes accessed | tf_op | source)
XLA Modules:
  0.0 206.4 jit_solution(4806828447603710436)
XLA Ops:
  0.6 0.0 copy-start
  0.6 1.4 broadcast_in_dim.35
  2.1 16.7 %all-to-all-start = ((bf16[8,40,128]{2,1,0:T(8,128)(2,1)}), bf16[8,40,128]{2,1,0:T(8,128)(2,1)S(1)}, u32[]{:S(2)}, u32[]{:S(2)}) async-start(bf16[8,40,128]{2,1,0:T(8,128)(2,1)} %broadcast_in_dim.35), calls=%async_computation | async-start | bytes 163840 | tf_op jit(solution)/shard_map/all_to_all | solution.py:27
  18.7 13.6 %all-gather = bf16[1,2,512,128]{3,2,1,0:T(8,128)(2,1)S(1)} all-gather(bf16[1,2,64,128]{3,2,1,0:T(8,128)(2,1)} %param.11), channel_id=2, replica_groups=mesh['kv'=8,'pb'=8,'rep'=8] {'rep'}, dimensions={2}, use_global_device_ids=true | all-gather | bytes 294912 | tf_op jit(solution)/shard_map/all_gather | solution.py:110
  32.3 0.0 copy-start.7
  32.3 1.4 copy.84
  33.7 0.0 copy-done.7
  33.7 0.1 broadcast_compare_fusion
  33.8 0.0 all-to-all-done
  33.9 0.5 fusion.26
  34.4 0.1 copy.63
  34.4 0.4 fusion.25
  34.8 0.1 copy.64
  34.9 0.3 fusion.4
  35.2 0.2 fusion.11
  35.5 0.2 fusion.5
  35.7 0.1 copy.66
  35.8 0.0 copy-start.3
  35.8 0.3 fusion.3
  36.2 32.5 %all_to_all.55 = bf16[8,48,128]{2,1,0:T(8,128)(2,1)S(1)} all-to-all(bf16[8,48,128]{2,1,0:T(8,128)(2,1)S(1)} %fusion.13), channel_id=1, replica_groups=mesh['kv'=8,'pb'=8,'rep'=8] {'pb'}, dimensions={0} | all-to-all | bytes 196608 | tf_op jit(solution)/shard_map/all_to_all | solution.py:27
  68.8 0.1 fusion.10
  68.9 0.0 copy-start.5
  68.9 9.3 %all_to_all.56 = bf16[8,40,128]{2,1,0:T(8,128)(2,1)S(1)} all-to-all(bf16[8,40,128]{2,1,0:T(8,128)(2,1)S(1)} %broadcast_in_dim.71), channel_id=1, replica_groups=mesh['kv'=8,'pb'=8,'rep'=8] {'rep'}, dimensions={0} | all-to-all | bytes 163840 | tf_op jit(solution)/shard_map/all_to_all | solution.py:27
  78.3 0.0 copy-done.3
  78.3 1.2 convolution_convert_fusion
  79.5 0.0 copy-start.4
  79.5 0.0 copy-done.5
  79.5 3.6 %all-to-all-start.3 = ((bf16[4,80,1024]{2,1,0:T(8,128)(2,1)}), bf16[4,80,1024]{2,1,0:T(8,128)(2,1)S(1)}, u32[]{:S(2)}, u32[]{:S(2)}) async-start(bf16[4,80,1024]{2,1,0:T(8,128)(2,1)} %bitcast.14), calls=%async_computation.3 | async-start | bytes 1310720 | tf_op jit(solution)/shard_map/all_to_all | solution.py:27
  83.1 11.0 %all-to-all-done.3 = bf16[4,80,1024]{2,1,0:T(8,128)(2,1)S(1)} async-done(((bf16[4,80,1024]{2,1,0:T(8,128)(2,1)}), bf16[4,80,1024]{2,1,0:T(8,128)(2,1)S(1)}, u32[]{:S(2)}, u32[]{:S(2)}) %all-to-all-start.3) | async-done | bytes 655392 | tf_op jit(solution)/shard_map/all_to_all | solution.py:27
  94.1 0.1 convert_reduce_fusion.2
  94.2 0.0 copy-start.6
  94.2 0.0 copy-done.4
  94.3 0.3 add.108
  94.6 0.7 copy.70
  95.3 3.5 %all-to-all-start.4 = ((bf16[16,40,128]{2,1,0:T(8,128)(2,1)}), bf16[16,40,128]{2,1,0:T(8,128)(2,1)S(1)}, u32[]{:S(2)}, u32[]{:S(2)}) async-start(bf16[16,40,128]{2,1,0:T(8,128)(2,1)} %bitcast.16), calls=%async_computation.4 | async-start | bytes 327680 | tf_op jit(solution)/shard_map/all_to_all | solution.py:27
  98.8 0.0 copy-done.6
  98.8 0.1 dynamic_slice.3
  98.9 14.1 %all-to-all-done.4 = bf16[16,40,128]{2,1,0:T(8,128)(2,1)S(1)} async-done(((bf16[16,40,128]{2,1,0:T(8,128)(2,1)}), bf16[16,40,128]{2,1,0:T(8,128)(2,1)S(1)}, u32[]{:S(2)}, u32[]{:S(2)}) %all-to-all-start.4) | async-done | bytes 163872 | tf_op jit(solution)/shard_map/all_to_all | solution.py:27
  113.0 18.3 %all_to_all.57 = bf16[16,40,128]{2,1,0:T(8,128)(2,1)S(1)} all-to-all(bf16[16,40,128]{2,1,0:T(8,128)(2,1)S(1)} %broadcast_in_dim.72), channel_id=1, replica_groups={{0,64,128,192,256,320,384,448,8,72,136,200,264,328,392,456},{16,80,144,..., dimensions={0} | all-to-all | bytes 327680 | tf_op jit(solution)/shard_map/all_to_all | solution.py:27
  131.3 0.9 broadcast_in_dim.74
  132.2 3.5 %all-to-all-start.6 = ((bf16[4,640,128]{2,1,0:T(8,128)(2,1)}), bf16[4,640,128]{2,1,0:T(8,128)(2,1)S(1)}, u32[]{:S(2)}, u32[]{:S(2)}) async-start(bf16[4,640,128]{2,1,0:T(8,128)(2,1)} %broadcast_in_dim.74), calls=%async_computation.6 | async-start | bytes 1310720 | tf_op jit(solution)/shard_map/all_to_all | solution.py:27
  135.7 8.7 %all-to-all-done.6 = bf16[4,640,128]{2,1,0:T(8,128)(2,1)S(1)} async-done(((bf16[4,640,128]{2,1,0:T(8,128)(2,1)}), bf16[4,640,128]{2,1,0:T(8,128)(2,1)S(1)}, u32[]{:S(2)}, u32[]{:S(2)}) %all-to-all-start.6) | async-done | bytes 655392 | tf_op jit(solution)/shard_map/all_to_all | solution.py:27
  144.4 0.0 copy-start.1
  144.4 0.0 copy-start.2
  144.4 0.1 copy.71
  144.5 0.1 copy.85
  144.7 1.0 copy-done.1
  145.6 0.3 copy-done.2
  145.9 0.9 shard_map.113
  146.8 14.2 %all_to_all.58 = bf16[8,40,1024]{2,1,0:T(8,128)(2,1)S(1)} all-to-all(bf16[8,40,1024]{2,1,0:T(8,128)(2,1)S(1)} %bitcast.70), channel_id=1, replica_groups=mesh['kv'=8,'pb'=8,'rep'=8] {'rep'}, dimensions={0} | all-to-all | bytes 1310720 | tf_op jit(solution)/shard_map/all_to_all | solution.py:27
  161.0 0.1 convert_reduce_fusion.1
  161.1 0.2 slice_reduce_fusion
  161.3 0.1 fusion.16
  161.5 10.6 %all_to_all.59 = bf16[8,40,462]{2,1,0:T(8,128)(2,1)S(1)} all-to-all(bf16[8,40,462]{2,1,0:T(8,128)(2,1)S(1)} %broadcast_in_dim.75), channel_id=1, replica_groups=mesh['kv'=8,'pb'=8,'rep'=8] {'rep'}, dimensions={0} | all-to-all | bytes 591360 | tf_op jit(solution)/shard_map/all_to_all | solution.py:27
  172.1 0.0 copy-done
  172.1 0.5 convolution_convert_fusion.1
  172.6 13.5 %all_to_all.60 = bf16[4,80,1024]{2,1,0:T(8,128)(2,1)S(1)} all-to-all(bf16[4,80,1024]{2,1,0:T(8,128)(2,1)S(1)} %bitcast.78), channel_id=1, replica_groups={{0,16,32,48},{8,24,40,56},{1,17,33,49},{9,25,41,57},{2,18,34,50},{10,26..., dimensions={0} | all-to-all | bytes 1310720 | tf_op jit(solution)/shard_map/all_to_all | solution.py:27
  186.1 0.1 convert_reduce_fusion
  186.2 0.1 convert_element_type.121
  186.3 19.4 %all_to_all.61 = bf16[16,40,128]{2,1,0:T(8,128)(2,1)S(1)} all-to-all(bf16[16,40,128]{2,1,0:T(8,128)(2,1)S(1)} %convert_element_type.121), channel_id=1, replica_groups={{0,64,128,192,256,320,384,448,8,72,136,200,264,328,392,456},{16,80,144,..., dimensions={0} | all-to-all | bytes 327680 | tf_op jit(solution)/shard_map/all_to_all | solution.py:27
  205.8 0.6 add.115
  (30 shorter events, 0.5 us)
Async XLA Ops:
  0.6 171.5 %copy-start = (bf16[462,1024]{1,0:T(8,128)(2,1)S(1)}, bf16[462,1024]{1,0:T(8,128)(2,1)}, u32[]{:S(2)}) copy-start(bf16[462,1024]{1,0:T(8,128)(2,1)} %param.19) | copy-start | bytes 2838532
  2.1 31.8 %all-to-all-start = ((bf16[8,40,128]{2,1,0:T(8,128)(2,1)}), bf16[8,40,128]{2,1,0:T(8,128)(2,1)S(1)}, u32[]{:S(2)}, u32[]{:S(2)}) async-start(bf16[8,40,128]{2,1,0:T(8,128)(2,1)} %broadcast_in_dim.35), calls=%async_computation | async-start | bytes 163840 | tf_op jit(solution)/shard_map/all_to_all | solution.py:27
  32.3 1.5 copy-start.7
  35.8 42.5 %copy-start.3 = (bf16[128,1024]{1,0:T(8,128)(2,1)S(1)}, bf16[128,1024]{1,0:T(8,128)(2,1)}, u32[]{:S(2)}) copy-start(bf16[128,1024]{1,0:T(8,128)(2,1)} %param.16) | copy-start | bytes 786436
  68.9 10.6 %copy-start.5 = (bf16[40,128]{1,0:T(8,128)(2,1)}, bf16[40,128]{1,0:T(8,128)(2,1)S(1)}, u32[]{:S(2)}) copy-start(bf16[40,128]{1,0:T(8,128)(2,1)S(1)} %fusion.10) | copy-start | bytes 30724
  79.5 14.8 %copy-start.4 = (f32[5,1024]{1,0:T(8,128)S(1)}, f32[5,1024]{1,0:T(8,128)}, u32[]{:S(2)}) copy-start(f32[5,1024]{1,0:T(8,128)} %param.14) | copy-start | bytes 61444
  79.5 14.6 %all-to-all-start.3 = ((bf16[4,80,1024]{2,1,0:T(8,128)(2,1)}), bf16[4,80,1024]{2,1,0:T(8,128)(2,1)S(1)}, u32[]{:S(2)}, u32[]{:S(2)}) async-start(bf16[4,80,1024]{2,1,0:T(8,128)(2,1)} %bitcast.14), calls=%async_computation.3 | async-start | bytes 1310720 | tf_op jit(solution)/shard_map/all_to_all | solution.py:27
  94.2 4.6 %copy-start.6 = (f32[1024]{0:T(1024)S(1)}, f32[1024]{0:T(1024)}, u32[]{:S(2)}) copy-start(f32[1024]{0:T(1024)} %param.15) | copy-start | bytes 12292
  95.3 17.6 %all-to-all-start.4 = ((bf16[16,40,128]{2,1,0:T(8,128)(2,1)}), bf16[16,40,128]{2,1,0:T(8,128)(2,1)S(1)}, u32[]{:S(2)}, u32[]{:S(2)}) async-start(bf16[16,40,128]{2,1,0:T(8,128)(2,1)} %bitcast.16), calls=%async_computation.4 | async-start | bytes 327680 | tf_op jit(solution)/shard_map/all_to_all | solution.py:27
  132.2 12.2 %all-to-all-start.6 = ((bf16[4,640,128]{2,1,0:T(8,128)(2,1)}), bf16[4,640,128]{2,1,0:T(8,128)(2,1)S(1)}, u32[]{:S(2)}, u32[]{:S(2)}) async-start(bf16[4,640,128]{2,1,0:T(8,128)(2,1)} %broadcast_in_dim.74), calls=%async_computation.6 | async-start | bytes 1310720 | tf_op jit(solution)/shard_map/all_to_all | solution.py:27
  144.4 1.2 copy-start.1
  144.4 1.5 copy-start.2

commit v3 on v2

--- a/solution.py
+++ b/solution.py
@@ -58,16 +58,54 @@
     return highest, denoms, numers
 
 
-def gate_up_body(rows_ref, inverse_gain_ref, gate_ref, up_ref, out_ref):
+def merge_body(at_ref, parts_ref, residual_ref, blocks_ref, total_ref):
+    total_ref[...] = sum(parts_ref[x].astype(f32) for x in range(X))
+    rows = total_ref.shape[0]
+    own = residual_ref.shape[0]
+    place = lax.broadcasted_iota(jnp.int32, (rows, 1), 0) - at_ref[0]
+    for j in range(Z // 2):
+        columns = slice(j * LANES, (j + 1) * LANES)
+        mixed = total_ref[:, columns]
+        for i in range(own):
+            mixed += jnp.where(place == i, residual_ref[i : i + 1, columns], 0.0)
+        for half in range(2):
+            blocks_ref[half * (Z // 2) + j] = mixed[
+                half * (rows // 2) : (half + 1) * (rows // 2)
+            ].astype(bf16)
+
+
+def merge(at, parts, residual):
+    _, rows, columns = parts.shape
+    vmem = pl.BlockSpec(memory_space=pltpu.VMEM)
+    return pl.pallas_call(
+        merge_body,
+        in_specs=[pl.BlockSpec(memory_space=pltpu.SMEM), vmem, vmem],
+        out_specs=(vmem, vmem),
+        out_shape=(
+            jax.ShapeDtypeStruct((Z, rows // 2, LANES), bf16),
+            jax.ShapeDtypeStruct((rows, columns), f32),
+        ),
+        compiler_params=pltpu.CompilerParams(vmem_limit_bytes=24 * 2**20),
+    )(at, parts, residual)
+
+
+def gate_up_body(blocks_ref, gain_ref, gate_ref, up_ref, out_ref, mixed_ref):
     units = gate_ref.shape[0]
+    tiles = mixed_ref.shape[1] // LANES
+    count = blocks_ref.shape[1]
+    for i in range(blocks_ref.shape[0] // tiles):
+        for j in range(tiles):
+            mixed_ref[i * count : (i + 1) * count, j * LANES : (j + 1) * LANES] = blocks_ref[
+                i * tiles + j
+            ].astype(f32)
+    mixed = mixed_ref[...]
+    squares = jnp.sum(mixed * mixed, axis=1, keepdims=True)
+    rows = (mixed * gain_ref[...]).astype(bf16)
     contract = (((1,), (1,)), ((), ()))
-    rows = rows_ref[...]
     gates = lax.dot_general(rows, gate_ref[...], contract, preferred_element_type=f32)
     out_ref[:, :units] = gates.astype(bf16)
     ups = lax.dot_general(rows, up_ref[...], contract, preferred_element_type=f32)
     out_ref[:, 512 : 512 + units] = ups.astype(bf16)
-    mixed = rows.astype(f32) * inverse_gain_ref[...]
-    squares = jnp.sum(mixed * mixed, axis=1, keepdims=True)
     high = squares.astype(bf16)
     squares = squares - high.astype(f32)
     middle = squares.astype(bf16)
@@ -76,14 +114,17 @@
         out_ref[:, units + i : units + i + 1] = value
 
 
-def gate_up(rows, inverse_gain, gates, ups):
+def gate_up(blocks, gain, gates, ups):
+    columns = gain.shape[0]
+    count = blocks.size // columns
     return pl.pallas_call(
         gate_up_body,
         in_specs=[pl.BlockSpec(memory_space=pltpu.VMEM)] * 4,
         out_specs=pl.BlockSpec(memory_space=pltpu.VMEM),
-        out_shape=jax.ShapeDtypeStruct((rows.shape[0], 1024), bf16),
+        out_shape=jax.ShapeDtypeStruct((count, 1024), bf16),
+        scratch_shapes=[pltpu.VMEM((count, columns), f32)],
         compiler_params=pltpu.CompilerParams(vmem_limit_bytes=24 * 2**20),
-    )(rows, inverse_gain, gates, ups)
+    )(blocks, gain[None], gates, ups)
 
 
 def per_device(
@@ -103,10 +144,7 @@
     part = rows // X
     own, columns = residual.shape
     z_at = lax.axis_index("pb") % ZH * 8 + lax.axis_index("kv")
-    own_rows = lax.dynamic_update_slice(
-        jnp.zeros((2 * rows, columns), f32), residual, (z_at * own, 0)
-    )
-    block_gain = lax.dynamic_slice(norm_gain, (z_at % 8 * LANES,), (LANES,))
+    own_at = (z_at * own)[None]
     prefix = lax.all_gather(prefix_cache[0], "rep", axis=1, tiled=True)
     group_queries = spread(queries[:, 0, :], 8, "pb")
     offset = lax.axis_index("pb") * suffix_cache.shape[3]
@@ -117,7 +155,8 @@
     logs = highest + jnp.log(denoms)
     stats = jnp.pad(jnp.stack(split_float(logs), axis=1), ((0, 0), (0, 5), (0, width - rows)))
     parts = (numers / denoms[..., None]).astype(bf16)
-    parts = exchange(jnp.concatenate([parts, stats], axis=1), "pb").astype(f32)
+    parts, own_at = lax.optimization_barrier((jnp.concatenate([parts, stats], axis=1), own_at))
+    parts = exchange(parts, "pb").astype(f32)
     logs = jnp.sum(parts[:, rows : rows + 3, :rows], axis=1)
     factor = jnp.exp(logs - jnp.max(logs, axis=0))
     factor = factor / jnp.sum(factor, axis=0)
@@ -126,16 +165,11 @@
     all_context = all_context.transpose(1, 2, 0, 3, 4).reshape(8 * rows, width)
     attended = jnp.dot(all_context, out_weight, preferred_element_type=f32).astype(bf16)
     attended = exchange(attended.reshape(X, 2 * rows, columns), "pb", x_groups)
-    attended = jnp.sum(attended.astype(f32), axis=0)
-    blocks = (attended + own_rows).astype(bf16).reshape(2, rows, Z // 2, LANES)
-    blocks = blocks.swapaxes(1, 2).reshape(Z, rows, LANES)
-    block = jnp.sum(exchange(blocks, ("kv", "pb"), z_groups).astype(f32), axis=0)
-    block = (block * block_gain).astype(bf16)
+    blocks, attended = merge(own_at, attended, residual)
+    block = jnp.sum(exchange(blocks, ("kv", "pb"), z_groups).astype(f32), axis=0).astype(bf16)
     sent = spread(block, Z, ("kv", "pb"), z_groups).reshape(-1, LANES)
-    sent = spread(sent, X, "pb", x_groups)
-    scaled = sent.reshape(2 * X, Z // 2, rows, LANES).swapaxes(1, 2)
-    scaled = scaled.reshape(8 * rows, columns)
-    partial = gate_up(scaled, 1.0 / norm_gain[None], gate_weight.T, up_weight.T)
+    sent = spread(sent, X, "pb", x_groups).reshape(-1, rows, LANES)
+    partial = gate_up(sent, norm_gain, gate_weight.T, up_weight.T)
     partial = exchange(partial.reshape(8, rows, 1024), "rep")
     summed = jnp.sum(partial.astype(f32), axis=0)
     inverse = lax.rsqrt(jnp.sum(summed[:, units : units + 3], axis=1, keepdims=True) / D + epsilon)

time: 207 us -> 200 us (0.966)
  blocking collectives: 131 us -> 173 us
  waiting for transfers between devices: 33.8 us -> 0.03 us
  starting transfers between devices: 27.2 us -> 16.7 us
  local copies, waits for them, and re-layouts: 6.8 us -> 3.43 us
    all_to_all x7 -> x10, blocking collectives: 118 us -> 159 us  [exchange(): lax.all_to_all(blocks, axes, 0, 0, axis_index_groups=groups, tiled=True)]
    all_to_all x4 -> x1, waiting for transfers between devices: 33.8 us -> 0.03 us  [exchange(): lax.all_to_all(blocks, axes, 0, 0, axis_index_groups=groups, tiled=True)]
    all_to_all x4 -> x1, starting transfers between devices: 27.2 us -> 16.7 us  [exchange(): lax.all_to_all(blocks, axes, 0, 0, axis_index_groups=groups, tiled=True)]
  transfers between devices with their start and end apart: 4 -> 1, of which waited for: 3 -> 0; matrix products, arithmetic and copies ran while one was open for 1% -> 1% of each run, Pallas kernels for 0% -> 0%
where the time goes in v3:
time: 200 us
  blocking collectives  173 us (86%)
  starting transfers between devices  16.7 us (8%)
  local copies, waits for them, and re-layouts  3.43 us (2%)
  matrix products  2.37 us (1%)
    all_to_all x10, blocking collectives, exchange(): lax.all_to_all(blocks, axes, 0, 0, axis_index_groups=groups, tiled=True)  159 us
    all_to_all x1, starting transfers between devices, exchange(): lax.all_to_all(blocks, axes, 0, 0, axis_index_groups=groups, tiled=True)  16.7 us
    all_gather x1, blocking collectives, per_device(): prefix = lax.all_gather(prefix_cache[0], 'rep', axis=1, tiled=True)  13.6 us
  transfers between devices with their start and end apart: 1, of which 0 were waited for; matrix products, arithmetic and copies ran while one was open for 1% of the time, Pallas kernels for 0%

profile of v3, /device:TPU:32, one launch (start us, length us, event | category | flops | bytes accessed | tf_op | source)
XLA Modules:
  0.0 199.5 jit_solution(12312360919745910110)
XLA Ops:
  0.6 0.0 copy-start
  0.6 1.4 broadcast_in_dim.69
  2.1 16.7 %all-to-all-start = ((bf16[8,40,128]{2,1,0:T(8,128)(2,1)}), bf16[8,40,128]{2,1,0:T(8,128)(2,1)S(1)}, u32[]{:S(2)}, u32[]{:S(2)}) async-start(bf16[8,40,128]{2,1,0:T(8,128)(2,1)} %broadcast_in_dim.69), calls=%async_computation | async-start | bytes 163840 | tf_op jit(solution)/shard_map/all_to_all | solution.py:27
  18.7 13.6 %all-gather = bf16[1,2,512,128]{3,2,1,0:T(8,128)(2,1)S(1)} all-gather(bf16[1,2,64,128]{3,2,1,0:T(8,128)(2,1)} %param.11), channel_id=2, replica_groups=mesh['kv'=8,'pb'=8,'rep'=8] {'rep'}, dimensions={2}, use_global_device_ids=true | all-gather | bytes 294912 | tf_op jit(solution)/shard_map/all_gather | solution.py:148
  32.3 0.0 copy-start.7
  32.3 1.4 copy.65
  33.7 0.0 copy-done.7
  33.7 0.1 broadcast_compare_fusion
  33.8 0.0 all-to-all-done
  33.9 0.5 fusion.26
  34.4 0.1 copy.49
  34.4 0.4 fusion.25
  34.8 0.1 copy.50
  34.9 0.3 fusion.4
  35.2 0.2 fusion.11
  35.5 0.2 fusion.5
  35.7 0.1 copy.52
  35.8 0.0 copy-start.5
  35.8 0.3 fusion.3
  36.2 32.5 %all_to_all.55 = bf16[8,48,128]{2,1,0:T(8,128)(2,1)S(1)} all-to-all(bf16[8,48,128]{2,1,0:T(8,128)(2,1)S(1)} %fusion.13), channel_id=1, replica_groups=mesh['kv'=8,'pb'=8,'rep'=8] {'pb'}, dimensions={0} | all-to-all | bytes 196608 | tf_op jit(solution)/shard_map/all_to_all | solution.py:27
  68.8 0.1 fusion.10
  68.9 0.0 copy-start.6
  68.9 9.3 %all_to_all.56 = bf16[8,40,128]{2,1,0:T(8,128)(2,1)S(1)} all-to-all(bf16[8,40,128]{2,1,0:T(8,128)(2,1)S(1)} %broadcast_in_dim.75), channel_id=1, replica_groups=mesh['kv'=8,'pb'=8,'rep'=8] {'rep'}, dimensions={0} | all-to-all | bytes 163840 | tf_op jit(solution)/shard_map/all_to_all | solution.py:27
  78.2 0.0 copy-start.3
  78.3 0.0 copy-done.5
  78.3 0.3 convolution_convert_fusion
  78.6 13.4 %all_to_all.57.parts_ref = bf16[4,80,1024]{2,1,0:T(8,128)(2,1)S(1)} all-to-all(bf16[4,80,1024]{2,1,0:T(8,128)(2,1)S(1)} %bitcast.61), channel_id=1, replica_groups={{0,16,32,48},{8,24,40,56},{1,17,33,49},{9,25,41,57},{2,18,34,50},{10,26..., dimensions={0} | all-to-all | bytes 1310720 | tf_op jit(solution)/shard_map/all_to_all | solution.py:27
  92.1 0.0 copy-done.6
  92.1 0.0 copy-done.3
  92.1 0.3 shard_map.113
  92.4 17.1 %all_to_all.58 = bf16[16,40,128]{2,1,0:T(8,128)(2,1)S(1)} all-to-all(bf16[16,40,128]{2,1,0:T(8,128)(2,1)S(1)} %get-tuple-element.8), channel_id=1, replica_groups={{0,64,128,192,256,320,384,448,8,72,136,200,264,328,392,456},{16,80,144,..., dimensions={0} | all-to-all | bytes 327680 | tf_op jit(solution)/shard_map/all_to_all | solution.py:27
  109.5 0.0 copy-start.1
  109.5 0.0 copy-start.2
  109.5 0.0 copy-start.4
  109.6 18.3 %all_to_all.59 = bf16[16,40,128]{2,1,0:T(8,128)(2,1)S(1)} all-to-all(bf16[16,40,128]{2,1,0:T(8,128)(2,1)S(1)} %broadcast_in_dim.76), channel_id=1, replica_groups={{0,64,128,192,256,320,384,448,8,72,136,200,264,328,392,456},{16,80,144,..., dimensions={0} | all-to-all | bytes 327680 | tf_op jit(solution)/shard_map/all_to_all | solution.py:27
  127.8 0.1 broadcast_in_dim.78
  127.9 11.2 %all_to_all.60 = bf16[4,640,128]{2,1,0:T(8,128)(2,1)S(1)} all-to-all(bf16[4,640,128]{2,1,0:T(8,128)(2,1)S(1)} %broadcast_in_dim.78), channel_id=1, replica_groups={{0,16,32,48},{8,24,40,56},{1,17,33,49},{9,25,41,57},{2,18,34,50},{10,26..., dimensions={0} | all-to-all | bytes 1310720 | tf_op jit(solution)/shard_map/all_to_all | solution.py:27
  139.1 0.0 copy-done.1
  139.1 0.0 copy-done.2
  139.1 0.0 copy-done.4
  139.1 0.9 shard_map.114
  140.0 14.2 %all_to_all.61 = bf16[8,40,1024]{2,1,0:T(8,128)(2,1)S(1)} all-to-all(bf16[8,40,1024]{2,1,0:T(8,128)(2,1)S(1)} %bitcast.55), channel_id=1, replica_groups=mesh['kv'=8,'pb'=8,'rep'=8] {'rep'}, dimensions={0} | all-to-all | bytes 1310720 | tf_op jit(solution)/shard_map/all_to_all | solution.py:27
  154.2 0.1 convert_reduce_fusion.1
  154.3 0.2 slice_reduce_fusion
  154.5 0.1 fusion.16
  154.7 10.6 %all_to_all.62 = bf16[8,40,462]{2,1,0:T(8,128)(2,1)S(1)} all-to-all(bf16[8,40,462]{2,1,0:T(8,128)(2,1)S(1)} %broadcast_in_dim.80), channel_id=1, replica_groups=mesh['kv'=8,'pb'=8,'rep'=8] {'rep'}, dimensions={0} | all-to-all | bytes 591360 | tf_op jit(solution)/shard_map/all_to_all | solution.py:27
  165.3 0.0 copy-done
  165.3 0.5 convolution_convert_fusion.1
  165.8 13.5 %all_to_all.63 = bf16[4,80,1024]{2,1,0:T(8,128)(2,1)S(1)} all-to-all(bf16[4,80,1024]{2,1,0:T(8,128)(2,1)S(1)} %bitcast.62), channel_id=1, replica_groups={{0,16,32,48},{8,24,40,56},{1,17,33,49},{9,25,41,57},{2,18,34,50},{10,26..., dimensions={0} | all-to-all | bytes 1310720 | tf_op jit(solution)/shard_map/all_to_all | solution.py:27
  179.3 0.1 convert_reduce_fusion
  179.4 0.1 reshape.208
  179.5 19.4 %all_to_all.64 = bf16[16,40,128]{2,1,0:T(8,128)(2,1)S(1)} all-to-all(bf16[16,40,128]{2,1,0:T(8,128)(2,1)S(1)} %reshape.208), channel_id=1, replica_groups={{0,64,128,192,256,320,384,448,8,72,136,200,264,328,392,456},{16,80,144,..., dimensions={0} | all-to-all | bytes 327680 | tf_op jit(solution)/shard_map/all_to_all | solution.py:27
  198.9 0.6 add.96
  (23 shorter events, 0.4 us)
Async XLA Ops:
  0.6 164.6 %copy-start = (bf16[462,1024]{1,0:T(8,128)(2,1)S(1)}, bf16[462,1024]{1,0:T(8,128)(2,1)}, u32[]{:S(2)}) copy-start(bf16[462,1024]{1,0:T(8,128)(2,1)} %param.19) | copy-start | bytes 2838532
  2.1 31.8 %all-to-all-start = ((bf16[8,40,128]{2,1,0:T(8,128)(2,1)}), bf16[8,40,128]{2,1,0:T(8,128)(2,1)S(1)}, u32[]{:S(2)}, u32[]{:S(2)}) async-start(bf16[8,40,128]{2,1,0:T(8,128)(2,1)} %broadcast_in_dim.69), calls=%async_computation | async-start | bytes 163840 | tf_op jit(solution)/shard_map/all_to_all | solution.py:27
  32.3 1.5 copy-start.7
  35.8 42.5 %copy-start.5 = (bf16[128,1024]{1,0:T(8,128)(2,1)S(1)}, bf16[128,1024]{1,0:T(8,128)(2,1)}, u32[]{:S(2)}) copy-start(bf16[128,1024]{1,0:T(8,128)(2,1)} %param.16) | copy-start | bytes 786436
  68.9 23.2 %copy-start.6 = (bf16[40,128]{1,0:T(8,128)(2,1)}, bf16[40,128]{1,0:T(8,128)(2,1)S(1)}, u32[]{:S(2)}) copy-start(bf16[40,128]{1,0:T(8,128)(2,1)S(1)} %fusion.10) | copy-start | bytes 30724
  78.2 13.8 %copy-start.3 = (f32[5,1024]{1,0:T(8,128)S(1)}, f32[5,1024]{1,0:T(8,128)}, u32[]{:S(2)}) copy-start(f32[5,1024]{1,0:T(8,128)} %residual_ref.1) | copy-start | bytes 61444
  109.5 29.6 %copy-start.1 = (bf16[1024,462]{0,1:T(8,128)(2,1)S(1)}, bf16[1024,462]{0,1:T(8,128)(2,1)}, u32[]{:S(2)}) copy-start(bf16[1024,462]{0,1:T(8,128)(2,1)} %param.17) | copy-start | bytes 2838532
  109.5 29.6 %copy-start.2 = (bf16[1024,462]{0,1:T(8,128)(2,1)S(1)}, bf16[1024,462]{0,1:T(8,128)(2,1)}, u32[]{:S(2)}) copy-start(bf16[1024,462]{0,1:T(8,128)(2,1)} %param.18) | copy-start | bytes 2838532
  109.5 29.6 %copy-start.4 = (f32[1024]{0:T(1024)S(1)}, f32[1024]{0:T(1024)}, u32[]{:S(2)}) copy-start(f32[1024]{0:T(1024)} %param.15) | copy-start | bytes 12292

commit v4 on v3

--- a/solution.py
+++ b/solution.py
@@ -41,20 +41,20 @@
 def local_attention(queries, prefix, suffix, lengths, offset):
     scale = HEAD_DIM ** (-0.5)
     heads, rows, width = queries.shape
+    count = suffix.shape[1] // 2
     shared = jnp.einsum("grd,td->grt", queries, prefix[0], preferred_element_type=f32) * scale
-    own = jnp.einsum("grd,rsd->grs", queries, suffix[:, 0], preferred_element_type=f32) * scale
-    position = offset + lax.broadcasted_iota(jnp.int32, (rows, suffix.shape[2]), 1)
-    is_live = (position < lengths[:, None])[None]
+    own = jnp.einsum("grd,rsd->grs", queries, suffix, preferred_element_type=f32) * scale
+    lane = lax.broadcasted_iota(jnp.int32, (rows, 2 * count), 1)
+    is_live = ((lane < count) & (offset + lane < lengths[:, None]))[None]
     own = jnp.where(is_live, own, lowest)
     highest = jnp.maximum(jnp.max(shared, axis=2), jnp.max(own, axis=2))
     shared_weights = jnp.exp(shared - highest[..., None])
     own_weights = jnp.where(is_live, jnp.exp(own - highest[..., None]), 0.0)
     denoms = jnp.sum(shared_weights, axis=2) + jnp.sum(own_weights, axis=2)
+    on_values = jnp.roll(own_weights.astype(bf16), count, axis=2)
     numers = jnp.einsum(
         "grt,td->grd", shared_weights.astype(bf16), prefix[1], preferred_element_type=f32
-    ) + jnp.einsum(
-        "grs,rsd->grd", own_weights.astype(bf16), suffix[:, 1], preferred_element_type=f32
-    )
+    ) + jnp.einsum("grs,rsd->grd", on_values, suffix, preferred_element_type=f32)
     return highest, denoms, numers
 
 
@@ -146,10 +146,15 @@
     z_at = lax.axis_index("pb") % ZH * 8 + lax.axis_index("kv")
     own_at = (z_at * own)[None]
     prefix = lax.all_gather(prefix_cache[0], "rep", axis=1, tiled=True)
-    group_queries = spread(queries[:, 0, :], 8, "pb")
+    mine = queries[:, 0, :]
+    other = lax.ppermute(mine, "pb", [(p, p ^ 1) for p in range(8)])
+    other, prefix = lax.optimization_barrier((other, prefix))
+    first = lax.axis_index("pb") % ZH == 0
+    pair = jnp.stack([jnp.where(first, mine, other), jnp.where(first, other, mine)])
+    group_queries = spread(pair, X, "pb", x_groups).reshape(8, rows, width)
     offset = lax.axis_index("pb") * suffix_cache.shape[3]
     highest, denoms, numers = local_attention(
-        group_queries, prefix, suffix_cache[:, 0], suffix_lengths, offset
+        group_queries, prefix, suffix_cache.reshape(rows, -1, width), suffix_lengths, offset
     )
 
     logs = highest + jnp.log(denoms)

time: 200 us -> 199 us (level)
  blocking collectives: 173 us -> 164 us
  waiting for transfers between devices: 0.03 us -> 4.99 us
  starting transfers between devices: 16.7 us -> 19.2 us
  local copies, waits for them, and re-layouts: 3.43 us -> 1.3 us
    ppermute x0 -> x1, starting transfers between devices: none -> 15 us  [per_device(): other = lax.ppermute(mine, 'pb', [(p, p ^ 1) for p in range(8)])]
    all_to_all x1, starting transfers between devices: 16.7 us -> 4.29 us  [exchange(): lax.all_to_all(blocks, axes, 0, 0, axis_index_groups=groups, tiled=True)]
    all_to_all x10, blocking collectives: 159 us -> 151 us  [exchange(): lax.all_to_all(blocks, axes, 0, 0, axis_index_groups=groups, tiled=True)]
    all_to_all x1, waiting for transfers between devices: 0.03 us -> 4.98 us  [exchange(): lax.all_to_all(blocks, axes, 0, 0, axis_index_groups=groups, tiled=True)]
  transfers between devices with their start and end apart: 1 -> 2, of which waited for: 0 -> 1; matrix products, arithmetic and copies ran while one was open for 1% -> 0% of each run, Pallas kernels for 0% -> 0%
where the time goes in v4:
time: 199 us; the launch traced here: 198 us
  blocking collectives  164 us (82%)
  starting transfers between devices  19.2 us (10%)
  waiting for transfers between devices  4.99 us (3%)
  other arithmetic  3.35 us (2%)
  matrix products  2.88 us (1%)
    all_to_all x10, blocking collectives, exchange(): lax.all_to_all(blocks, axes, 0, 0, axis_index_groups=groups, tiled=True)  151 us
    ppermute x1, starting transfers between devices, per_device(): other = lax.ppermute(mine, 'pb', [(p, p ^ 1) for p in range(8)])  15 us
    all_gather x1, blocking collectives, per_device(): prefix = lax.all_gather(prefix_cache[0], 'rep', axis=1, tiled=True)  13.6 us
    all_to_all x1, waiting for transfers between devices, exchange(): lax.all_to_all(blocks, axes, 0, 0, axis_index_groups=groups, tiled=True)  4.98 us
    all_to_all x1, starting transfers between devices, exchange(): lax.all_to_all(blocks, axes, 0, 0, axis_index_groups=groups, tiled=True)  4.29 us
  transfers between devices with their start and end apart: 2, of which 1 were waited for; matrix products, arithmetic and copies ran while one was open for 0% of the time, Pallas kernels for 0%

profile of v4, /device:TPU:32, one launch (start us, length us, event | category | flops | bytes accessed | tf_op | source)
XLA Modules:
  0.0 198.3 jit_solution(16028283907373933575)
XLA Ops:
  0.6 0.0 copy-start
  0.6 15.0 %collective-permute-start = (bf16[40,128]{1,0:T(8,128)(2,1)}, bf16[40,128]{1,0:T(8,128)(2,1)S(1)}, u32[]{:S(2)}, u32[]{:S(2)}) collective-permute-start(bf16[40,128]{1,0:T(8,128)(2,1)} %bitcast.69), channel_id=1, source_target_pairs={{0,8},{8,0},{16,24},{24,16},{32,40},{40,32},{48,56},{56,48},{1,9},... | collective-permute-start | bytes 30728 | tf_op jit(solution)/shard_map/ppermute | solution.py:150
  15.6 13.6 %all-gather = bf16[1,2,512,128]{3,2,1,0:T(8,128)(2,1)S(1)} all-gather(bf16[1,2,64,128]{3,2,1,0:T(8,128)(2,1)} %param.11), channel_id=2, replica_groups=mesh['kv'=8,'pb'=8,'rep'=8] {'rep'}, dimensions={2}, use_global_device_ids=true | all-gather | bytes 294912 | tf_op jit(solution)/shard_map/all_gather | solution.py:148
  29.2 0.0 collective-permute-done
  29.2 0.7 select_bitcast_fusion.1
  29.9 0.6 broadcast_in_dim.36
  30.6 4.3 %all-to-all-start = ((bf16[4,2,40,128]{3,2,1,0:T(8,128)(2,1)}), bf16[4,2,40,128]{3,2,1,0:T(8,128)(2,1)S(1)}, u32[]{:S(2)}, u32[]{:S(2)}) async-start(bf16[4,2,40,128]{3,2,1,0:T(8,128)(2,1)} %broadcast_in_dim.36), calls=%async_computation | async-start | bytes 163840 | tf_op jit(solution)/shard_map/all_to_all | solution.py:27
  34.9 0.7 compare_and_fusion
  35.6 5.0 %all-to-all-done = bf16[4,2,40,128]{3,2,1,0:T(8,128)(2,1)S(1)} async-done(((bf16[4,2,40,128]{3,2,1,0:T(8,128)(2,1)}), bf16[4,2,40,128]{3,2,1,0:T(8,128)(2,1)S(1)}, u32[]{:S(2)}, u32[]{:S(2)}) %all-to-all-start) | async-done | bytes 81952 | tf_op jit(solution)/shard_map/all_to_all | solution.py:27
  40.6 0.0 copy-done
  40.6 0.9 fusion.30
  41.4 0.1 copy.43
  41.5 0.4 fusion.29
  41.9 0.1 copy.44
  42.0 0.2 fusion.4
  42.2 0.2 fusion.11
  42.4 0.1 copy.46
  42.5 0.1 fusion.28
  42.6 0.5 fusion.19
  43.1 0.0 copy-start.6
  43.1 0.3 fusion.3
  43.5 17.6 %all_to_all.55 = bf16[8,48,128]{2,1,0:T(8,128)(2,1)S(1)} all-to-all(bf16[8,48,128]{2,1,0:T(8,128)(2,1)S(1)} %fusion.16), channel_id=1, replica_groups=mesh['kv'=8,'pb'=8,'rep'=8] {'pb'}, dimensions={0} | all-to-all | bytes 196608 | tf_op jit(solution)/shard_map/all_to_all | solution.py:27
  61.2 0.1 fusion.9
  61.3 0.0 copy-start.7
  61.4 9.3 %all_to_all.56 = bf16[8,40,128]{2,1,0:T(8,128)(2,1)S(1)} all-to-all(bf16[8,40,128]{2,1,0:T(8,128)(2,1)S(1)} %broadcast_in_dim.73), channel_id=1, replica_groups=mesh['kv'=8,'pb'=8,'rep'=8] {'rep'}, dimensions={0} | all-to-all | bytes 163840 | tf_op jit(solution)/shard_map/all_to_all | solution.py:27
  70.7 0.0 copy-start.3
  70.8 0.0 copy-done.6
  70.8 0.3 convolution_convert_fusion
  71.1 13.4 %all_to_all.57.parts_ref = bf16[4,80,1024]{2,1,0:T(8,128)(2,1)S(1)} all-to-all(bf16[4,80,1024]{2,1,0:T(8,128)(2,1)S(1)} %bitcast.59), channel_id=1, replica_groups={{0,16,32,48},{8,24,40,56},{1,17,33,49},{9,25,41,57},{2,18,34,50},{10,26..., dimensions={0} | all-to-all | bytes 1310720 | tf_op jit(solution)/shard_map/all_to_all | solution.py:27
  84.5 0.0 copy-done.7
  84.5 0.0 copy-done.3
  84.6 0.3 shard_map.113
  84.8 23.4 %all_to_all.58 = bf16[16,40,128]{2,1,0:T(8,128)(2,1)S(1)} all-to-all(bf16[16,40,128]{2,1,0:T(8,128)(2,1)S(1)} %get-tuple-element.12), channel_id=1, replica_groups={{0,64,128,192,256,320,384,448,8,72,136,200,264,328,392,456},{16,80,144,..., dimensions={0} | all-to-all | bytes 327680 | tf_op jit(solution)/shard_map/all_to_all | solution.py:27
  108.3 0.0 copy-start.1
  108.3 0.0 copy-start.2
  108.3 0.0 copy-start.4
  108.3 18.3 %all_to_all.59 = bf16[16,40,128]{2,1,0:T(8,128)(2,1)S(1)} all-to-all(bf16[16,40,128]{2,1,0:T(8,128)(2,1)S(1)} %broadcast_in_dim.74), channel_id=1, replica_groups={{0,64,128,192,256,320,384,448,8,72,136,200,264,328,392,456},{16,80,144,..., dimensions={0} | all-to-all | bytes 327680 | tf_op jit(solution)/shard_map/all_to_all | solution.py:27
  126.6 0.1 broadcast_in_dim.76
  126.7 11.2 %all_to_all.60 = bf16[4,640,128]{2,1,0:T(8,128)(2,1)S(1)} all-to-all(bf16[4,640,128]{2,1,0:T(8,128)(2,1)S(1)} %broadcast_in_dim.76), channel_id=1, replica_groups={{0,16,32,48},{8,24,40,56},{1,17,33,49},{9,25,41,57},{2,18,34,50},{10,26..., dimensions={0} | all-to-all | bytes 1310720 | tf_op jit(solution)/shard_map/all_to_all | solution.py:27
  137.9 0.0 copy-done.1
  137.9 0.0 copy-done.2
  137.9 0.0 copy-done.4
  137.9 0.9 shard_map.114
  138.8 14.2 %all_to_all.61 = bf16[8,40,1024]{2,1,0:T(8,128)(2,1)S(1)} all-to-all(bf16[8,40,1024]{2,1,0:T(8,128)(2,1)S(1)} %bitcast.55), channel_id=1, replica_groups=mesh['kv'=8,'pb'=8,'rep'=8] {'rep'}, dimensions={0} | all-to-all | bytes 1310720 | tf_op jit(solution)/shard_map/all_to_all | solution.py:27
  153.0 0.0 copy-start.5
  153.0 0.1 convert_reduce_fusion.1
  153.1 0.2 slice_reduce_fusion
  153.3 0.1 fusion.18
  153.4 10.6 %all_to_all.62 = bf16[8,40,462]{2,1,0:T(8,128)(2,1)S(1)} all-to-all(bf16[8,40,462]{2,1,0:T(8,128)(2,1)S(1)} %broadcast_in_dim.78), channel_id=1, replica_groups=mesh['kv'=8,'pb'=8,'rep'=8] {'rep'}, dimensions={0} | all-to-all | bytes 591360 | tf_op jit(solution)/shard_map/all_to_all | solution.py:27
  164.0 0.0 copy-done.5
  164.0 0.5 convolution_convert_fusion.1
  164.6 13.5 %all_to_all.63 = bf16[4,80,1024]{2,1,0:T(8,128)(2,1)S(1)} all-to-all(bf16[4,80,1024]{2,1,0:T(8,128)(2,1)S(1)} %bitcast.60), channel_id=1, replica_groups={{0,16,32,48},{8,24,40,56},{1,17,33,49},{9,25,41,57},{2,18,34,50},{10,26..., dimensions={0} | all-to-all | bytes 1310720 | tf_op jit(solution)/shard_map/all_to_all | solution.py:27
  178.1 0.1 convert_reduce_fusion
  178.2 0.1 reshape.230
  178.3 19.4 %all_to_all.64 = bf16[16,40,128]{2,1,0:T(8,128)(2,1)S(1)} all-to-all(bf16[16,40,128]{2,1,0:T(8,128)(2,1)S(1)} %reshape.230), channel_id=1, replica_groups={{0,64,128,192,256,320,384,448,8,72,136,200,264,328,392,456},{16,80,144,..., dimensions={0} | all-to-all | bytes 327680 | tf_op jit(solution)/shard_map/all_to_all | solution.py:27
  197.7 0.6 add.97
  (25 shorter events, 0.4 us)
Async XLA Ops:
  0.6 39.9 %copy-start = (bf16[40,1,2,64,128]{4,3,2,1,0:T(8,128)(2,1)S(1)}, bf16[40,1,2,64,128]{4,3,2,1,0:T(8,128)(2,1)}, u32[]{:S(2)}) copy-start(bf16[40,1,2,64,128]{4,3,2,1,0:T(8,128)(2,1)} %param.12) | copy-start | bytes 3932164
  0.6 28.6 %collective-permute-start = (bf16[40,128]{1,0:T(8,128)(2,1)}, bf16[40,128]{1,0:T(8,128)(2,1)S(1)}, u32[]{:S(2)}, u32[]{:S(2)}) collective-permute-start(bf16[40,128]{1,0:T(8,128)(2,1)} %bitcast.69), channel_id=1, source_target_pairs={{0,8},{8,0},{16,24},{24,16},{32,40},{40,32},{48,56},{56,48},{1,9},... | collective-permute-start | bytes 30728 | tf_op jit(solution)/shard_map/ppermute | solution.py:150
  30.6 10.0 %all-to-all-start = ((bf16[4,2,40,128]{3,2,1,0:T(8,128)(2,1)}), bf16[4,2,40,128]{3,2,1,0:T(8,128)(2,1)S(1)}, u32[]{:S(2)}, u32[]{:S(2)}) async-start(bf16[4,2,40,128]{3,2,1,0:T(8,128)(2,1)} %broadcast_in_dim.36), calls=%async_computation | async-start | bytes 163840 | tf_op jit(solution)/shard_map/all_to_all | solution.py:27
  43.1 27.6 %copy-start.6 = (bf16[128,1024]{1,0:T(8,128)(2,1)S(1)}, bf16[128,1024]{1,0:T(8,128)(2,1)}, u32[]{:S(2)}) copy-start(bf16[128,1024]{1,0:T(8,128)(2,1)} %param.16) | copy-start | bytes 786436
  61.3 23.2 %copy-start.7 = (bf16[40,128]{1,0:T(8,128)(2,1)}, bf16[40,128]{1,0:T(8,128)(2,1)S(1)}, u32[]{:S(2)}) copy-start(bf16[40,128]{1,0:T(8,128)(2,1)S(1)} %fusion.9) | copy-start | bytes 30724
  70.7 13.8 %copy-start.3 = (f32[5,1024]{1,0:T(8,128)S(1)}, f32[5,1024]{1,0:T(8,128)}, u32[]{:S(2)}) copy-start(f32[5,1024]{1,0:T(8,128)} %residual_ref.1) | copy-start | bytes 61444
  108.3 29.6 %copy-start.1 = (bf16[1024,462]{0,1:T(8,128)(2,1)S(1)}, bf16[1024,462]{0,1:T(8,128)(2,1)}, u32[]{:S(2)}) copy-start(bf16[1024,462]{0,1:T(8,128)(2,1)} %param.17) | copy-start | bytes 2838532
  108.3 29.6 %copy-start.2 = (bf16[1024,462]{0,1:T(8,128)(2,1)S(1)}, bf16[1024,462]{0,1:T(8,128)(2,1)}, u32[]{:S(2)}) copy-start(bf16[1024,462]{0,1:T(8,128)(2,1)} %param.18) | copy-start | bytes 2838532
  108.3 29.6 %copy-start.4 = (f32[1024]{0:T(1024)S(1)}, f32[1024]{0:T(1024)}, u32[]{:S(2)}) copy-start(f32[1024]{0:T(1024)} %param.15) | copy-start | bytes 12292
  153.0 11.1 %copy-start.5 = (bf16[462,1024]{1,0:T(8,128)(2,1)S(1)}, bf16[462,1024]{1,0:T(8,128)(2,1)}, u32[]{:S(2)}) copy-start(bf16[462,1024]{1,0:T(8,128)(2,1)} %param.19) | copy-start | bytes 2838532

commit v5 on v4

--- a/solution.py
+++ b/solution.py
@@ -38,18 +38,16 @@
     return high.astype(bf16), middle.astype(bf16), (rest - middle).astype(bf16)
 
 
-def local_attention(queries, prefix, suffix, lengths, offset):
+def local_attention(queries, prefix, suffix, lane_bias):
     scale = HEAD_DIM ** (-0.5)
     heads, rows, width = queries.shape
     count = suffix.shape[1] // 2
     shared = jnp.einsum("grd,td->grt", queries, prefix[0], preferred_element_type=f32) * scale
     own = jnp.einsum("grd,rsd->grs", queries, suffix, preferred_element_type=f32) * scale
-    lane = lax.broadcasted_iota(jnp.int32, (rows, 2 * count), 1)
-    is_live = ((lane < count) & (offset + lane < lengths[:, None]))[None]
-    own = jnp.where(is_live, own, lowest)
+    own = own + lane_bias[None]
     highest = jnp.maximum(jnp.max(shared, axis=2), jnp.max(own, axis=2))
     shared_weights = jnp.exp(shared - highest[..., None])
-    own_weights = jnp.where(is_live, jnp.exp(own - highest[..., None]), 0.0)
+    own_weights = jnp.exp(own - highest[..., None])
     denoms = jnp.sum(shared_weights, axis=2) + jnp.sum(own_weights, axis=2)
     on_values = jnp.roll(own_weights.astype(bf16), count, axis=2)
     numers = jnp.einsum(
@@ -148,19 +146,25 @@
     prefix = lax.all_gather(prefix_cache[0], "rep", axis=1, tiled=True)
     mine = queries[:, 0, :]
     other = lax.ppermute(mine, "pb", [(p, p ^ 1) for p in range(8)])
-    other, prefix = lax.optimization_barrier((other, prefix))
+    slots = suffix_cache.shape[3]
+    lane = lax.broadcasted_iota(jnp.int32, (rows, 2 * slots), 1)
+    position = lax.axis_index("pb") * slots + lane
+    is_live = (lane < slots) & (position < suffix_lengths[:, None])
+    lane_bias = jnp.where(is_live, 0.0, lowest).astype(f32)
+    other, prefix, lane_bias, own_at = lax.optimization_barrier(
+        (other, prefix, lane_bias, own_at)
+    )
     first = lax.axis_index("pb") % ZH == 0
     pair = jnp.stack([jnp.where(first, mine, other), jnp.where(first, other, mine)])
     group_queries = spread(pair, X, "pb", x_groups).reshape(8, rows, width)
-    offset = lax.axis_index("pb") * suffix_cache.shape[3]
     highest, denoms, numers = local_attention(
-        group_queries, prefix, suffix_cache.reshape(rows, -1, width), suffix_lengths, offset
+        group_queries, prefix, suffix_cache.reshape(rows, -1, width), lane_bias
     )
 
     logs = highest + jnp.log(denoms)
     stats = jnp.pad(jnp.stack(split_float(logs), axis=1), ((0, 0), (0, 5), (0, width - rows)))
     parts = (numers / denoms[..., None]).astype(bf16)
-    parts, own_at = lax.optimization_barrier((jnp.concatenate([parts, stats], axis=1), own_at))
+    parts = jnp.concatenate([parts, stats], axis=1)
     parts = exchange(parts, "pb").astype(f32)
     logs = jnp.sum(parts[:, rows : rows + 3, :rows], axis=1)
     factor = jnp.exp(logs - jnp.max(logs, axis=0))

time: 199 us -> 199 us (level)
  blocking collectives: 164 us -> 174 us
  waiting for transfers between devices: 4.99 us -> 0.01 us
  starting transfers between devices: 19.2 us -> 15 us
    all_to_all x10 -> x11, blocking collectives: 151 us -> 161 us  [exchange(): lax.all_to_all(blocks, axes, 0, 0, axis_index_groups=groups, tiled=True)]
    all_to_all x1 -> x0, waiting for transfers between devices: 4.98 us -> none  [exchange(): lax.all_to_all(blocks, axes, 0, 0, axis_index_groups=groups, tiled=True)]
    all_to_all x1 -> x0, starting transfers between devices: 4.29 us -> none  [exchange(): lax.all_to_all(blocks, axes, 0, 0, axis_index_groups=groups, tiled=True)]
  transfers between devices with their start and end apart: 2 -> 1, of which waited for: 1 -> 0; matrix products, arithmetic and copies ran while one was open for 0% -> 0% of each run, Pallas kernels for 0% -> 0%
where the time goes in v5:
time: 199 us; the launch traced here: 198 us
  blocking collectives  174 us (87%)
  starting transfers between devices  15 us (8%)
  other arithmetic  3.35 us (2%)
  matrix products  2.89 us (1%)
    all_to_all x11, blocking collectives, exchange(): lax.all_to_all(blocks, axes, 0, 0, axis_index_groups=groups, tiled=True)  161 us
    ppermute x1, starting transfers between devices, per_device(): other = lax.ppermute(mine, 'pb', [(p, p ^ 1) for p in range(8)])  15 us
    all_gather x1, blocking collectives, per_device(): prefix = lax.all_gather(prefix_cache[0], 'rep', axis=1, tiled=True)  13.6 us
  transfers between devices with their start and end apart: 1, of which 0 were waited for; matrix products, arithmetic and copies ran while one was open for 0% of the time, Pallas kernels for 0%

profile of v5, /device:TPU:32, one launch (start us, length us, event | category | flops | bytes accessed | tf_op | source)
XLA Modules:
  0.0 198.2 jit_solution(13708969386824177375)
XLA Ops:
  0.6 0.0 copy-start
  0.6 15.0 %collective-permute-start = (bf16[40,128]{1,0:T(8,128)(2,1)}, bf16[40,128]{1,0:T(8,128)(2,1)S(1)}, u32[]{:S(2)}, u32[]{:S(2)}) collective-permute-start(bf16[40,128]{1,0:T(8,128)(2,1)} %bitcast.76), channel_id=1, source_target_pairs={{0,8},{8,0},{16,24},{24,16},{32,40},{40,32},{48,56},{56,48},{1,9},... | collective-permute-start | bytes 30728 | tf_op jit(solution)/shard_map/ppermute | solution.py:148
  15.6 0.7 and_select_fusion
  16.4 13.6 %all-gather = bf16[1,2,512,128]{3,2,1,0:T(8,128)(2,1)S(1)} all-gather(bf16[1,2,64,128]{3,2,1,0:T(8,128)(2,1)} %param.11), channel_id=2, replica_groups=mesh['kv'=8,'pb'=8,'rep'=8] {'rep'}, dimensions={2}, use_global_device_ids=true | all-gather | bytes 294912 | tf_op jit(solution)/shard_map/all_gather | solution.py:146
  29.9 0.0 collective-permute-done
  29.9 0.7 select_bitcast_fusion.1
  30.7 9.8 %all_to_all.55 = bf16[4,2,40,128]{3,2,1,0:T(8,128)(2,1)S(1)} all-to-all(bf16[4,2,40,128]{3,2,1,0:T(8,128)(2,1)S(1)} %broadcast_in_dim.27), channel_id=1, replica_groups={{0,16,32,48},{8,24,40,56},{1,17,33,49},{9,25,41,57},{2,18,34,50},{10,26..., dimensions={0} | all-to-all | bytes 163840 | tf_op jit(solution)/shard_map/all_to_all | solution.py:27
  40.5 0.0 copy-done
  40.5 0.9 bitcast_reduce_fusion
  41.3 0.1 copy.43
  41.4 0.4 fusion.28
  41.8 0.1 copy.44
  41.9 0.2 fusion.2
  42.1 0.2 fusion.10
  42.3 0.1 copy.46
  42.4 0.1 fusion.27
  42.5 0.5 fusion.18
  43.0 0.0 copy-start.6
  43.0 0.3 fusion.1
  43.4 17.6 %all_to_all.56 = bf16[8,48,128]{2,1,0:T(8,128)(2,1)S(1)} all-to-all(bf16[8,48,128]{2,1,0:T(8,128)(2,1)S(1)} %fusion.15), channel_id=1, replica_groups=mesh['kv'=8,'pb'=8,'rep'=8] {'pb'}, dimensions={0} | all-to-all | bytes 196608 | tf_op jit(solution)/shard_map/all_to_all | solution.py:27
  61.1 0.1 fusion.7
  61.3 0.0 copy-start.7
  61.3 9.3 %all_to_all.57 = bf16[8,40,128]{2,1,0:T(8,128)(2,1)S(1)} all-to-all(bf16[8,40,128]{2,1,0:T(8,128)(2,1)S(1)} %broadcast_in_dim.28), channel_id=1, replica_groups=mesh['kv'=8,'pb'=8,'rep'=8] {'rep'}, dimensions={0} | all-to-all | bytes 163840 | tf_op jit(solution)/shard_map/all_to_all | solution.py:27
  70.6 0.0 copy-start.3
  70.7 0.0 copy-done.6
  70.7 0.3 convolution_convert_fusion
  71.0 13.4 %all_to_all.58.parts_ref = bf16[4,80,1024]{2,1,0:T(8,128)(2,1)S(1)} all-to-all(bf16[4,80,1024]{2,1,0:T(8,128)(2,1)S(1)} %bitcast.66), channel_id=1, replica_groups={{0,16,32,48},{8,24,40,56},{1,17,33,49},{9,25,41,57},{2,18,34,50},{10,26..., dimensions={0} | all-to-all | bytes 1310720 | tf_op jit(solution)/shard_map/all_to_all | solution.py:27
  84.5 0.0 copy-done.7
  84.5 0.0 copy-done.3
  84.5 0.3 shard_map.113
  84.7 23.4 %all_to_all.59 = bf16[16,40,128]{2,1,0:T(8,128)(2,1)S(1)} all-to-all(bf16[16,40,128]{2,1,0:T(8,128)(2,1)S(1)} %get-tuple-element.12), channel_id=1, replica_groups={{0,64,128,192,256,320,384,448,8,72,136,200,264,328,392,456},{16,80,144,..., dimensions={0} | all-to-all | bytes 327680 | tf_op jit(solution)/shard_map/all_to_all | solution.py:27
  108.2 0.0 copy-start.1
  108.2 0.0 copy-start.2
  108.2 0.0 copy-start.4
  108.2 18.3 %all_to_all.60 = bf16[16,40,128]{2,1,0:T(8,128)(2,1)S(1)} all-to-all(bf16[16,40,128]{2,1,0:T(8,128)(2,1)S(1)} %broadcast_in_dim.29), channel_id=1, replica_groups={{0,64,128,192,256,320,384,448,8,72,136,200,264,328,392,456},{16,80,144,..., dimensions={0} | all-to-all | bytes 327680 | tf_op jit(solution)/shard_map/all_to_all | solution.py:27
  126.5 0.1 broadcast_in_dim.31
  126.6 11.2 %all_to_all.61 = bf16[4,640,128]{2,1,0:T(8,128)(2,1)S(1)} all-to-all(bf16[4,640,128]{2,1,0:T(8,128)(2,1)S(1)} %broadcast_in_dim.31), channel_id=1, replica_groups={{0,16,32,48},{8,24,40,56},{1,17,33,49},{9,25,41,57},{2,18,34,50},{10,26..., dimensions={0} | all-to-all | bytes 1310720 | tf_op jit(solution)/shard_map/all_to_all | solution.py:27
  137.8 0.0 copy-done.1
  137.8 0.0 copy-done.2
  137.8 0.0 copy-done.4
  137.8 0.9 shard_map.114
  138.7 14.2 %all_to_all.62 = bf16[8,40,1024]{2,1,0:T(8,128)(2,1)S(1)} all-to-all(bf16[8,40,1024]{2,1,0:T(8,128)(2,1)S(1)} %bitcast.62), channel_id=1, replica_groups=mesh['kv'=8,'pb'=8,'rep'=8] {'rep'}, dimensions={0} | all-to-all | bytes 1310720 | tf_op jit(solution)/shard_map/all_to_all | solution.py:27
  152.9 0.0 copy-start.5
  152.9 0.1 convert_reduce_fusion.1
  153.0 0.2 slice_reduce_fusion
  153.2 0.1 fusion.17
  153.3 10.6 %all_to_all.63 = bf16[8,40,462]{2,1,0:T(8,128)(2,1)S(1)} all-to-all(bf16[8,40,462]{2,1,0:T(8,128)(2,1)S(1)} %broadcast_in_dim.33), channel_id=1, replica_groups=mesh['kv'=8,'pb'=8,'rep'=8] {'rep'}, dimensions={0} | all-to-all | bytes 591360 | tf_op jit(solution)/shard_map/all_to_all | solution.py:27
  164.0 0.0 copy-done.5
  164.0 0.5 convolution_convert_fusion.1
  164.5 13.5 %all_to_all.64 = bf16[4,80,1024]{2,1,0:T(8,128)(2,1)S(1)} all-to-all(bf16[4,80,1024]{2,1,0:T(8,128)(2,1)S(1)} %bitcast.67), channel_id=1, replica_groups={{0,16,32,48},{8,24,40,56},{1,17,33,49},{9,25,41,57},{2,18,34,50},{10,26..., dimensions={0} | all-to-all | bytes 1310720 | tf_op jit(solution)/shard_map/all_to_all | solution.py:27
  178.0 0.1 convert_reduce_fusion
  178.1 0.1 reshape.193
  178.2 19.4 %all_to_all.65 = bf16[16,40,128]{2,1,0:T(8,128)(2,1)S(1)} all-to-all(bf16[16,40,128]{2,1,0:T(8,128)(2,1)S(1)} %reshape.193), channel_id=1, replica_groups={{0,64,128,192,256,320,384,448,8,72,136,200,264,328,392,456},{16,80,144,..., dimensions={0} | all-to-all | bytes 327680 | tf_op jit(solution)/shard_map/all_to_all | solution.py:27
  197.6 0.6 add.111
  (26 shorter events, 0.4 us)
Async XLA Ops:
  0.6 39.9 %copy-start = (bf16[40,1,2,64,128]{4,3,2,1,0:T(8,128)(2,1)S(1)}, bf16[40,1,2,64,128]{4,3,2,1,0:T(8,128)(2,1)}, u32[]{:S(2)}) copy-start(bf16[40,1,2,64,128]{4,3,2,1,0:T(8,128)(2,1)} %param.12) | copy-start | bytes 3932164
  0.6 29.3 %collective-permute-start = (bf16[40,128]{1,0:T(8,128)(2,1)}, bf16[40,128]{1,0:T(8,128)(2,1)S(1)}, u32[]{:S(2)}, u32[]{:S(2)}) collective-permute-start(bf16[40,128]{1,0:T(8,128)(2,1)} %bitcast.76), channel_id=1, source_target_pairs={{0,8},{8,0},{16,24},{24,16},{32,40},{40,32},{48,56},{56,48},{1,9},... | collective-permute-start | bytes 30728 | tf_op jit(solution)/shard_map/ppermute | solution.py:148
  43.0 27.6 %copy-start.6 = (bf16[128,1024]{1,0:T(8,128)(2,1)S(1)}, bf16[128,1024]{1,0:T(8,128)(2,1)}, u32[]{:S(2)}) copy-start(bf16[128,1024]{1,0:T(8,128)(2,1)} %param.16) | copy-start | bytes 786436
  61.3 23.2 %copy-start.7 = (bf16[40,128]{1,0:T(8,128)(2,1)}, bf16[40,128]{1,0:T(8,128)(2,1)S(1)}, u32[]{:S(2)}) copy-start(bf16[40,128]{1,0:T(8,128)(2,1)S(1)} %fusion.7) | copy-start | bytes 30724
  70.6 13.8 %copy-start.3 = (f32[5,1024]{1,0:T(8,128)S(1)}, f32[5,1024]{1,0:T(8,128)}, u32[]{:S(2)}) copy-start(f32[5,1024]{1,0:T(8,128)} %residual_ref.1) | copy-start | bytes 61444
  108.2 29.6 %copy-start.1 = (bf16[1024,462]{0,1:T(8,128)(2,1)S(1)}, bf16[1024,462]{0,1:T(8,128)(2,1)}, u32[]{:S(2)}) copy-start(bf16[1024,462]{0,1:T(8,128)(2,1)} %param.17) | copy-start | bytes 2838532
  108.2 29.6 %copy-start.2 = (bf16[1024,462]{0,1:T(8,128)(2,1)S(1)}, bf16[1024,462]{0,1:T(8,128)(2,1)}, u32[]{:S(2)}) copy-start(bf16[1024,462]{0,1:T(8,128)(2,1)} %param.18) | copy-start | bytes 2838532
  108.2 29.6 %copy-start.4 = (f32[1024]{0:T(1024)S(1)}, f32[1024]{0:T(1024)}, u32[]{:S(2)}) copy-start(f32[1024]{0:T(1024)} %param.15) | copy-start | bytes 12292
  152.9 11.1 %copy-start.5 = (bf16[462,1024]{1,0:T(8,128)(2,1)S(1)}, bf16[462,1024]{1,0:T(8,128)(2,1)}, u32[]{:S(2)}) copy-start(bf16[462,1024]{1,0:T(8,128)(2,1)} %param.19) | copy-start | bytes 2838532
